TPU v7x, 256 devices: a whole 4x4x8 slice. The times are simulated.
256 devices in a mesh: seq: 32 (over z_hi, y, core), tensor: 4 (over x), dp: 2 (over z_lo).
Axes of the slice: x: 4, y: 4, z: 8 (z_hi: 4, z_lo: 2; z = z_hi * 2 + z_lo), core: 2. Of those that a mesh axis runs over, the one named last changes fastest.
Arguments:
- hidden_in: bfloat16 [2, 32, 256, 1152], P('dp', 'seq'), may hold values from -6 to 6
- norm1_gain: float32 [1152], replicated, may hold values from 0.1 to 1.9
- qkv_weight: bfloat16 [1152, 3, 1152], P(None, None, 'tensor'), may hold values from -0.25043365 to 0.25043365
- out_weight: bfloat16 [1152, 1152], P('tensor'), may hold values from -0.1875 to 0.1875
- norm2_gain: float32 [1152], replicated, may hold values from 0.1 to 1.9
- fc1_weight: bfloat16 [1152, 4608], P(None, 'tensor'), may hold values from -0.1875 to 0.1875
- fc2_weight: bfloat16 [1152, 4608], P(None, 'tensor'), may hold values from -0.09375 to 0.09375
- out_grad: bfloat16 [2, 32, 256, 1152], P('dp', 'seq'), may hold values from -8 to 8
Outputs:
- block_out: bfloat16 [2, 32, 256, 1152], P('dp', 'seq')
- grad_mid: bfloat16 [2, 32, 256, 1152], P('dp', 'seq')
- grad_fc1: float32 [1152, 4608], P(('seq', 'dp'), 'tensor')
- grad_fc2: float32 [1152, 4608], P(('seq', 'dp'), 'tensor')
All inputs are finite; a program needn't handle non-finite values.
Results may differ from a plain program's by a relative error of at most 0.0077.
Values may be sent and summed in bfloat16 or wider, within the bound.
A program may use at most 128 MiB of HBM per device.

v0:
```python
import jax
import jax.numpy as jnp
from jax import lax
from jax.sharding import PartitionSpec as P

HDIM = 72


epsilon = 1e-06


def normalize(values):
    values = values.astype(jnp.float32)
    center = values - jnp.mean(values, -1, keepdims=True)
    inv_std = lax.rsqrt(jnp.mean(center * center, -1, keepdims=True) + epsilon)
    return (center * inv_std, inv_std)


def gelu_tanh(values):
    return jax.nn.gelu(values, approximate=True)


def norm_back(grad_norm, x_hat, inv_std, gain, upstream):
    scaled = grad_norm * gain
    plain_mean = jnp.mean(scaled, -1, keepdims=True)
    cross_mean = jnp.mean(scaled * x_hat, -1, keepdims=True)
    total = upstream.astype(jnp.float32) + inv_std * (scaled - plain_mean - x_hat * cross_mean)
    return total.astype(jnp.bfloat16)


def attend(queries, keys_all, values_all):
    scores = jnp.einsum(
        "bfphd,bgphd->bphfg", queries, keys_all, preferred_element_type=jnp.float32
    ) * HDIM ** (-0.5)
    shifted = scores - jnp.max(scores, -1, keepdims=True)
    weights = jnp.exp(shifted)
    probs = (weights / jnp.sum(weights, -1, keepdims=True)).astype(jnp.bfloat16)
    result = jnp.einsum("bphfg,bgphd->bfphd", probs, values_all, preferred_element_type=jnp.float32)
    return result.astype(jnp.bfloat16)


def contract_last(left, right):
    return lax.dot_general(
        left, right, (((1,), (1,)), ((), ())), preferred_element_type=jnp.float32
    )


def contract_first(left, right):
    return lax.dot_general(
        left, right, (((0,), (0,)), ((), ())), preferred_element_type=jnp.float32
    )


def local(
    hidden_in, norm1_gain, qkv_weight, out_weight, norm2_gain, fc1_weight, fc2_weight, out_grad
):
    clip_count, frames_here, patches, feature = hidden_in.shape
    head_cols = qkv_weight.shape[2]
    heads_here = head_cols // HDIM
    hidden_cols = fc1_weight.shape[1]
    tok_rows = clip_count * frames_here * patches
    flat_in = hidden_in.reshape(tok_rows, feature)
    x_hat1, _ = normalize(flat_in)
    norm_a = (x_hat1 * norm1_gain).astype(jnp.bfloat16)
    qkv = jnp.dot(
        norm_a, qkv_weight.reshape(feature, 3 * head_cols), preferred_element_type=jnp.float32
    ).astype(jnp.bfloat16)
    qkv = qkv.reshape(clip_count, frames_here, patches, 3, head_cols)
    block = lax.all_to_all(qkv, "seq", split_axis=2, concat_axis=1, tiled=True)
    count = block.shape[0]
    all_frames = block.shape[1]
    patch_here = block.shape[2]
    split = block.reshape(count, all_frames, patch_here, 3, heads_here, HDIM)
    result = attend(split[:, :, :, 0], split[:, :, :, 1], split[:, :, :, 2])
    result = result.reshape(count, all_frames, patch_here, head_cols)
    attended = lax.all_to_all(result, "seq", split_axis=1, concat_axis=2, tiled=True)
    attended = attended.reshape(tok_rows, head_cols)
    grad_flat = out_grad.reshape(tok_rows, feature)
    share_rows = tok_rows // lax.axis_size("tensor")
    share_start = lax.axis_index("tensor") * share_rows
    proj_share = lax.psum_scatter(
        jnp.dot(attended, out_weight, preferred_element_type=jnp.float32),
        "tensor",
        scatter_dimension=0,
        tiled=True,
    )
    in_share = lax.dynamic_slice_in_dim(flat_in, share_start, share_rows, 0)
    mid_share = (in_share.astype(jnp.float32) + proj_share).astype(jnp.bfloat16)
    x_hat2, inv_std2 = normalize(mid_share)
    norm_share = (x_hat2 * norm2_gain).astype(jnp.bfloat16)
    norm_b, mid = (
        lax.all_gather(norm_share, "tensor", axis=0, tiled=True),
        lax.all_gather(mid_share, "tensor", axis=0, tiled=True),
    )
    pre = jnp.dot(norm_b, fc1_weight, preferred_element_type=jnp.float32)
    act_full, gelu_grad = jax.vjp(gelu_tanh, pre)
    act = act_full.astype(jnp.bfloat16)
    down_share = lax.psum_scatter(
        contract_last(act, fc2_weight), "tensor", scatter_dimension=0, tiled=True
    )
    block_share = (mid_share.astype(jnp.float32) + down_share).astype(jnp.bfloat16)
    grad_act = jnp.dot(grad_flat, fc2_weight, preferred_element_type=jnp.float32)
    grad_pre = gelu_grad(grad_act)[0].astype(jnp.bfloat16)
    grad_norm_share = lax.psum_scatter(
        contract_last(grad_pre, fc1_weight), "tensor", scatter_dimension=0, tiled=True
    )
    grad_in_share = lax.dynamic_slice_in_dim(grad_flat, share_start, share_rows, 0)
    grad_mid_share = norm_back(grad_norm_share, x_hat2, inv_std2, norm2_gain, grad_in_share)
    block_flat, grad_mid_flat = (
        lax.all_gather(block_share, "tensor", axis=0, tiled=True),
        lax.all_gather(grad_mid_share, "tensor", axis=0, tiled=True),
    )
    both = lax.psum_scatter(
        jnp.concatenate([contract_first(norm_b, grad_pre), contract_first(grad_flat, act)], 1),
        ("seq", "dp"),
        scatter_dimension=0,
        tiled=True,
    )
    grad_fc1 = both[:, :hidden_cols]
    grad_fc2 = both[:, hidden_cols:]
    shape = hidden_in.shape
    return (block_flat.reshape(shape), grad_mid_flat.reshape(shape), grad_fc1, grad_fc2)


def solution(mesh):
    return jax.shard_map(
        local,
        mesh=mesh,
        in_specs=(
            P("dp", "seq", None, None),
            P(),
            P(None, None, "tensor"),
            P("tensor", None),
            P(),
            P(None, "tensor"),
            P(None, "tensor"),
            P("dp", "seq", None, None),
        ),
        out_specs=(
            P("dp", "seq", None, None),
            P("dp", "seq", None, None),
            P(("seq", "dp"), "tensor"),
            P(("seq", "dp"), "tensor"),
        ),
        check_vma=False,
    )
```

profile of v0, /device:TPU:1, one launch (start us, length us, event | category | flops | bytes accessed | tf_op | source)
XLA Modules:
  0.0 401.7 jit_solution(16025760269235055671)
XLA Ops:
  7.2 0.0 reduce-scatter.5.cloned.1.call-start
  7.2 1.4 convert_reduce_fusion
  8.6 1.4 fusion.15
  10.0 3.2 convolution_convert_fusion
  13.2 1.5 copy.23
  14.7 35.3 %all_to_all.8 = bf16[1,1,256,3,288]{4,3,1,0,2:T(4,128)(2,1)} all-to-all(bf16[1,1,256,3,288]{4,3,1,0,2:T(4,128)(2,1)S(1)} %copy.23), channel_id=1, replica_groups=mesh['seq'=32,'tensor'=4,'dp'=2] {'seq'}, dimensions={2} | all-to-all | bytes 884736 | tf_op jit(solution)/shard_map/all_to_all | solution.py:69
  50.0 2.6 reshape.151
  52.6 1.1 fusion.49
  53.7 1.4 fusion.50
  55.1 0.3 fusion.16
  55.4 0.1 copy.29
  55.5 0.2 reshape.141
  55.7 17.3 %all_to_all.9 = bf16[1,32,8,288]{3,2,0,1:T(8,128)(2,1)S(1)} all-to-all(bf16[1,32,8,288]{3,2,0,1:T(8,128)(2,1)S(1)} %bitcast.77), channel_id=1, replica_groups=mesh['seq'=32,'tensor'=4,'dp'=2] {'seq'}, dimensions={1} | all-to-all | bytes 294912 | tf_op jit(solution)/shard_map/all_to_all | solution.py:76
  73.0 2.6 fusion.42
  75.6 0.0 reduce-scatter.5.cloned.1.call-update
  75.6 0.0 reduce-scatter.9.cloned.1.call-start
  75.6 21.0 %reduce-scatter.5.cloned.1.call-done = f32[64,1152]{1,0:T(8,128)} async-done(((f32[256,1152]{1,0:T(8,128)}), f32[64,1152]{1,0:T(8,128)}) %reduce-scatter.5.cloned.1.call-update) | async-done | bytes 294928 | tf_op jit(solution)/shard_map/reduce_scatter | solution.py:81
  96.6 1.1 convert_reduce_fusion.1
  97.8 0.2 fusion.38
  98.0 0.1 fusion.32
  98.1 10.7 %all_gather.9 = bf16[256,1152]{1,0:T(8,128)(2,1)S(1)} all-gather(bf16[64,1152]{1,0:T(8,128)(2,1)S(1)} %fusion.32), channel_id=1, replica_groups=mesh['seq'=32,'tensor'=4,'dp'=2] {'tensor'}, dimensions={0}, use_global_device_ids=true | all-gather | bytes 737280 | tf_op jit(solution)/shard_map/all_gather | solution.py:92
  108.9 1.0 fusion.51
  109.9 1.0 copy-done.2
  110.9 1.4 fusion.9
  112.3 0.8 copy-done.7
  113.1 2.1 fusion.52
  115.2 0.0 reduce-scatter.9.cloned.1.call-update
  115.2 0.0 reduce-scatter.7.cloned.1.call-start
  115.2 4.3 %fusion.46 = f32[256,1152]{1,0:T(8,128)} fusion(bf16[1152,1152]{1,0:T(8,128)(2,1)} %param.14, f32[256,1152]{1,0:T(8,128)} %copy-done.2), kind=kOutput, calls=%fused_computation.70 | convolution fusion | flops 682131456 | bytes 5013504 | tf_op jit(solution)/shard_map/dot_general | solution.py:43
  119.5 0.2 all-reduce.3.cloned.1.call-start
  119.8 4.5 %fusion.53 = f32[1152,1152]{0,1:T(8,128)} fusion(bf16[256,1152]{1,0:T(8,128)(2,1)S(1)} %all_gather.9, bf16[256,1152]{1,0:T(8,128)(2,1)} %copy-done.7), kind=kOutput, calls=%fused_computation.76 | convolution fusion | flops 679477248 | bytes 6488064 | tf_op jit(solution)/shard_map/dot_general | solution.py:49
  124.3 3.5 convolution_bitcast_fusion
  127.8 9.0 %pad_maximum_fusion = f32[1152,2304]{0,1:T(8,128)} fusion(f32[1152,1152]{0,1:T(8,128)} %convolution_bitcast_fusion, f32[1152,1152]{0,1:T(8,128)} %fusion.53), kind=kLoop, calls=%fused_computation.1 | loop fusion | flops 2654208 | bytes 21233664 | tf_op jit(solution)/shard_map/concatenate | solution.py:114
  136.8 0.6 copy-done.12
  137.5 0.6 dynamic-slice.2
  138.7 5.6 %reduce-scatter.9.cloned.1.call-done = f32[64,1152]{1,0:T(8,128)} async-done(((f32[256,1152]{1,0:T(8,128)}), f32[64,1152]{1,0:T(8,128)}) %reduce-scatter.9.cloned.1.call-update) | async-done | bytes 294928 | tf_op jit(solution)/shard_map/reduce_scatter | solution.py:104
  144.3 1.2 multiply_reduce_fusion
  145.6 27.8 %reduce-scatter.7.cloned.1.call-done = f32[64,1152]{1,0:T(8,128)} async-done(((f32[256,1152]{1,0:T(8,128)}), f32[64,1152]{1,0:T(8,128)}) %reduce-scatter.7.cloned.1.call-update) | async-done | bytes 294928 | tf_op jit(solution)/shard_map/reduce_scatter | solution.py:98
  173.3 1.3 fusion.37
  174.6 10.7 %all_gather.10 = bf16[256,1152]{1,0:T(8,128)(2,1)S(1)} all-gather(bf16[64,1152]{1,0:T(8,128)(2,1)S(1)} %get-tuple-element.26), channel_id=1, replica_groups=mesh['seq'=32,'tensor'=4,'dp'=2] {'tensor'}, dimensions={0}, use_global_device_ids=true | all-gather | bytes 737280 | tf_op jit(solution)/shard_map/all_gather | solution.py:110
  185.3 11.3 %all_gather.11 = bf16[256,1152]{1,0:T(8,128)(2,1)} all-gather(bf16[64,1152]{1,0:T(8,128)(2,1)S(1)} %get-tuple-element.25), channel_id=1, replica_groups=mesh['seq'=32,'tensor'=4,'dp'=2] {'tensor'}, dimensions={0}, use_global_device_ids=true | all-gather | bytes 737280 | tf_op jit(solution)/shard_map/all_gather | solution.py:111
  196.6 189.5 %all-reduce.3.cloned.1.call-done = f32[1152,2304]{0,1:T(8,128)} async-done(((f32[1152,2304]{0,1:T(8,128)}), f32[1152,2304]{0,1:T(8,128)}) %all-reduce.3.cloned.1.call-update) | async-done | bytes 10616848
  386.2 3.0 fusion.48
  389.2 1.9 copy.31
  391.1 1.9 copy.32
  393.0 0.8 copy.62
  393.9 0.5 copy-done.4
  394.3 0.8 copy.63
  (29 shorter events, 0.1 us)
Async XLA Ops:
  7.2 101.7 %copy-start = (bf16[1152,1152]{1,0:T(8,128)(2,1)S(1)}, bf16[1152,1152]{1,0:T(8,128)(2,1)}, u32[]{:S(2)}) copy-start(bf16[1152,1152]{1,0:T(8,128)(2,1)} %param.13) | copy-start | bytes 7962628
  7.2 2.8 copy-start.1
  7.2 2.8 copy-start.11
  7.2 89.4 %reduce-scatter.5.cloned.1.call-start = ((), (), s32[]{:S(2)}) async-start(), calls=%async_computation.5 | async-start | bytes 1474560 | tf_op jit(solution)/shard_map/reduce_scatter | solution.py:81
  53.7 1.4 copy-start.8
  75.6 22.4 %copy-start.9 = (f32[1152]{0:T(1024)S(1)}, f32[1152]{0:T(1024)}, u32[]{:S(2)}) copy-start(f32[1152]{0:T(1024)} %param.12) | copy-start | bytes 13828
  75.6 68.8 %reduce-scatter.9.cloned.1.call-start = ((), (), s32[]{:S(2)}) async-start(), calls=%async_computation.7 | async-start | bytes 1474560 | tf_op jit(solution)/shard_map/reduce_scatter | solution.py:104
  108.9 2.0 copy-start.5
  108.9 2.0 copy-start.10
  109.9 1.0 copy-start.2
  112.3 0.8 copy-start.7
  115.2 58.1 %reduce-scatter.7.cloned.1.call-start = ((), (), s32[]{:S(2)}) async-start(), calls=%async_computation.6 | async-start | bytes 1474560 | tf_op jit(solution)/shard_map/reduce_scatter | solution.py:98
  119.5 266.6 %all-reduce.3.cloned.1.call-start = ((), (), s32[]{:S(2)}) async-start(), calls=%async_computation.8 | async-start | bytes 21233664
  119.8 4.6 %copy-start.3 = (f32[256,1152]{1,0:T(8,128)S(1)}, f32[256,1152]{1,0:T(8,128)}, u32[]{:S(2)}) copy-start(f32[256,1152]{1,0:T(8,128)} %copy-done.2) | copy-start | bytes 3538948
  119.8 4.6 %copy-start.6 = (bf16[1,1,256,1152]{3,2,1,0:T(8,128)(2,1)S(1)}, bf16[1,1,256,1152]{3,2,1,0:T(8,128)(2,1)}, u32[]{:S(2)}) copy-start(bf16[1,1,256,1152]{3,2,1,0:T(8,128)(2,1)} %param.15) | copy-start | bytes 1769476
  136.8 0.7 copy-start.12
  393.0 1.3 copy-start.4
Sparse Core Ops, SparseCore 0:
  75.7 20.8 reduce-scatter.4
  115.3 28.9 reduce-scatter.8
  146.9 26.3 reduce-scatter.6
  176.8 209.3 all-reduce.2
where the time goes:
time: 403 us; the launch traced here: 402 us
  waiting for transfers between devices  244 us (61%)
  blocking collectives  85.4 us (21%)
  matrix products  24.2 us (6%)
  local copies, waits for them, and re-layouts  17.5 us (4%)
  other arithmetic  15.7 us (4%)
  between operations  14.6 us (4%)
    unnamed x5, waiting for transfers between devices  190 us
    all_to_all x1, blocking collectives, local(): block = lax.all_to_all(qkv, 'seq', split_axis=2, concat_axis=1, tiled=True)  35.3 us
    reduce_scatter x1, waiting for transfers between devices, local(): lax.psum_scatter(contract_last(act, fc2_weight), 'tensor', scatter_dimens...  27.8 us
    reduce_scatter x1, waiting for transfers between devices, local(): lax.psum_scatter(jnp.dot(attended, out_weight, preferred_element_type=jnp...  21 us
    all_to_all x1, blocking collectives, local(): lax.all_to_all(result, 'seq', split_axis=1, concat_axis=2, tiled=True)  17.3 us
    all_gather x1, blocking collectives, local(): lax.all_gather(grad_mid_share, 'tensor', axis=0, tiled=True)  11.3 us
    all_gather x1, blocking collectives, local(): lax.all_gather(norm_share, 'tensor', axis=0, tiled=True)  10.7 us
    all_gather x1, blocking collectives, local(): lax.all_gather(block_share, 'tensor', axis=0, tiled=True)  10.7 us
  transfers between devices with their start and end apart: 4, of which 4 were waited for; matrix products, arithmetic and copies ran while one was open for 6% of the time, Pallas kernels for 0%

commit v1 on v0

v1 whole, which is shorter than its diff:
```python
import functools

import jax
import jax.numpy as jnp
import numpy as np
from jax import lax
from jax.experimental import pallas as pl
from jax.experimental.pallas import tpu as pltpu
from jax.sharding import PartitionSpec as P

MESH = pl.DeviceIdType.MESH
BF16 = jnp.bfloat16
F32 = jnp.float32

HDIM = 72
D = 1152
FQ = 1152
QC = 288
SLAB = 40
ROWS = 32 * SLAB
CA = 640
CB = 512
EPS = 1e-06
N_SEM = 160


def slab_sources():
    source = np.full((8, 4, SLAB), -1, np.int32)
    for z in range(8):
        for y in range(4):
            for core in range(2):
                first = ((z // 2) * 8 + y * 2 + core) * 36 + (z % 2) * 18
                source[z, y, core * 18 : core * 18 + 18] = np.arange(first, first + 18)
    return np.broadcast_to(source.reshape(1, ROWS), (8, ROWS)).copy()


def nn(a, b):
    return jnp.dot(a, b, preferred_element_type=F32)


def nt(a, b):
    return lax.dot_general(a, b, (((1,), (1,)), ((), ())), preferred_element_type=F32)


def normalize(values):
    center = values - jnp.mean(values, -1, keepdims=True)
    inv_std = lax.rsqrt(jnp.mean(center * center, -1, keepdims=True) + EPS)
    return center * inv_std, inv_std


def kernel(
    hid, gain1, wq_h, wo_h, gain2, w1_h, w2_h, og, idx,
    out_b, out_g, out_1, out_2,
    hs, gs, wq, wo, w1, w2, na, att, gflat, ga, act, gp, nb,
    pf, pb, xr1, xs2, xq, mid, xhat, inv2, bo, go,
    perm, nbp, gpp, lp, rp, lt,
    wa, ya1, yas, yaq, ra, za1, zas, zaq,
    wb, zb1, zbs, zbq, rb, yb1, ybs, ybq, fin,
    ssem, rsem, lsem, asem,
):
    t = lax.axis_index("tensor")
    s = lax.axis_index("seq")
    dp = lax.axis_index("dp")
    zh = s // 8
    y = (s // 2) % 4
    core = s % 2
    zz = zh * 2 + dp

    def wrap(value, size):
        return (value + 2 * size) % size

    def x_dev(step):
        return {"tensor": wrap(t + step, 4)}

    def y_dev(step):
        return {"seq": zh * 8 + wrap(y + step, 4) * 2 + core}

    def z_dev(step):
        other = wrap(zz + step, 8)
        return {"seq": (other // 2) * 8 + y * 2 + core, "dp": other % 2}

    core_dev = {"seq": s + 1 - 2 * core}

    def peer_seq(plane, a, k):
        return a * 8 + wrap(plane - zh - y - a, 4) * 2 + k

    barrier = pltpu.get_barrier_semaphore()
    for dev in (x_dev(1), x_dev(-1), y_dev(1), y_dev(-1), z_dev(1), z_dev(-1), core_dev):
        pl.semaphore_signal(barrier, inc=1, device_id=dev, device_id_type=MESH)
    for a in range(4):
        for k in range(2):
            peer = peer_seq(t, a, k)

            pl.semaphore_signal(barrier, inc=1, device_id={"seq": peer}, device_id_type=MESH)

    loads = [
        pltpu.make_async_copy(src, dst, lsem.at[i])
        for i, (src, dst) in enumerate(((wq_h, wq), (w2_h, w2), (wo_h, wo), (w1_h, w1)))
    ]
    for load in loads:
        load.start()
    pl.semaphore_wait(barrier, 15)

    count = [0]
    started = []

    def fresh(n=1):
        first = count[0]
        count[0] += n
        return first

    def send(src, dst, dev):
        i = fresh()
        copy = pltpu.make_async_remote_copy(
            src_ref=src, dst_ref=dst, send_sem=ssem.at[i], recv_sem=rsem.at[i], device_id=dev, device_id_type=MESH
        )
        copy.start()
        started.append(copy)
        return copy

    def exchange(src_of, dst, base):
        for a in range(4):
            for k in range(2):
                j = a * 2 + k
                peer = peer_seq(t, a, k)
                src = src_of(j, peer)

                @pl.when(peer != s)
                def _():
                    pltpu.make_async_remote_copy(
                        src_ref=src, dst_ref=dst, send_sem=ssem.at[base + j], recv_sem=rsem.at[base + zh * 2 + core],
                        device_id={"seq": peer}, device_id_type=MESH,
                    ).start()

                @pl.when(peer == s)
                def _():
                    pltpu.make_async_copy(src, dst, rsem.at[base + j]).start()

    def exchange_arrived(dst, base, j):
        pltpu.make_async_copy(dst, dst, rsem.at[base + j]).wait()

    def exchange_sent(src_of, base):
        for a in range(4):
            for k in range(2):
                j = a * 2 + k
                peer = peer_seq(t, a, k)
                src = src_of(j, peer)

                @pl.when(peer != s)
                def _():
                    pltpu.make_async_copy(src, src, ssem.at[base + j]).wait()

    base_h, base_g, base_b, base_gm = fresh(8), fresh(8), fresh(8), fresh(8)
    here = hs.at[t, zh * 2 + core]
    exchange(lambda j, peer: hid.at[peer], here, base_h)
    exchange(lambda j, peer: og.at[peer], gs.at[t, zh * 2 + core], base_g)

    def gather_first(view, arrived):
        copies = []
        for a in range(4):
            arrived(a)
            copies.append(
                (send(view(t, a), view(t, a), x_dev(1)), send(view(t, a), view(t, a), x_dev(-1)))
            )
        return copies

    def gather_second(view, copies):
        left, right = wrap(t - 1, 4), wrap(t + 1, 4)
        further = []
        for a in range(2):
            copies[a][0].wait_recv()
            further.append(send(view(left, a), view(left, a), x_dev(1)))
            copies[a + 2][1].wait_recv()
            further.append(send(view(right, a + 2), view(right, a + 2), x_dev(-1)))
        for a in range(2):
            copies[a + 2][0].wait_recv()
            copies[a][1].wait_recv()
        return further

    def gather_third(further):
        for copy in further:
            copy.wait_recv()

    def pair(ref):
        return lambda plane, a: ref.at[plane, pl.ds(a * 2, 2)]

    def slabs_arrived(dst, base):
        def arrived(a):
            for k in range(2):
                exchange_arrived(dst, base, a * 2 + k)

        return arrived

    def make_perm(i, carry):
        first = pl.multiple_of(i * 128, 128)
        row = lax.broadcasted_iota(jnp.int32, (128, ROWS), 0) + first
        perm[pl.ds(first, 128), :] = jnp.where(row == idx[0:1, :], 1.0, 0.0).astype(BF16)
        return carry

    lax.fori_loop(0, 9, make_perm, 0)

    g1 = gain1[0:1, :]

    def norm_share(plane):
        x_hat, _ = normalize(hs[plane].astype(F32).reshape(64, D))
        na[plane] = (x_hat * g1).astype(BF16)

    h_first = gather_first(pair(hs), slabs_arrived(here, base_h))
    norm_share(t)
    h_further = gather_second(pair(hs), h_first)
    norm_share(wrap(t - 1, 4))
    norm_share(wrap(t + 1, 4))
    g_first = gather_first(pair(gs), slabs_arrived(here, base_g))
    gather_third(h_further)
    norm_share(wrap(t + 2, 4))

    loads[0].wait()
    na_all = na[...].reshape(256, D)
    q = nt(na_all, wq[0:QC, :]).astype(BF16)
    k_ = nt(na_all, wq[QC : 2 * QC, :]).astype(BF16)
    v = nt(na_all, wq[2 * QC : 3 * QC, :]).astype(BF16)
    col = lax.broadcasted_iota(jnp.int32, (1, QC), 1)
    same = (lax.broadcasted_iota(jnp.int32, (256, 256), 0) & 7) == (lax.broadcasted_iota(jnp.int32, (256, 256), 1) & 7)
    total = jnp.zeros((256, QC), F32)
    for h in range(QC // HDIM):
        mine = (col >= h * HDIM) & (col < (h + 1) * HDIM)
        qh = jnp.where(mine, q, jnp.zeros_like(q))
        scores = nt(qh, k_) * HDIM ** (-0.5)
        scores = jnp.where(same, scores, -1e30)
        weights = jnp.exp(scores - jnp.max(scores, -1, keepdims=True))
        probs = (weights * (1.0 / jnp.sum(weights, -1, keepdims=True))).astype(BF16)
        total = jnp.where(mine, nn(probs, v), total)
    att[...] = total.astype(BF16)
    loads[2].wait()

    def partial_sums(u, product):
        for n in range(3):
            value = product(n)
            pf[u, :, :, n * 384 : n * 384 + 384] = value.reshape(4, 64, 384)
            pb[u, :, :, n * 384 : n * 384 + 384] = value.astype(BF16).reshape(4, 64, 384)

    def reduce_first(u):
        far, right, left = wrap(t + 2, 4), wrap(t + 1, 4), wrap(t - 1, 4)
        lo, hi = pl.ds(0, 32), pl.ds(32, 32)
        r1 = send(pb.at[u, far, lo], xr1.at[u, 0], x_dev(1))
        l1 = send(pb.at[u, far, hi], xr1.at[u, 1], x_dev(-1))
        r2 = send(pb.at[u, right, hi], xq.at[u, 0, hi], x_dev(1))
        l2 = send(pb.at[u, left, lo], xq.at[u, 1, lo], x_dev(-1))
        return r1, l1, r2, l2

    def reduce_second(u, copies):
        right, left = wrap(t + 1, 4), wrap(t - 1, 4)
        lo, hi = pl.ds(0, 32), pl.ds(32, 32)
        r1, l1, r2, l2 = copies
        r1.wait_recv()
        xs2[u, 0] = (pf[u, right, 0:32, :] + xr1[u, 0].astype(F32)).astype(BF16)
        r3 = send(xs2.at[u, 0], xq.at[u, 0, lo], x_dev(1))
        l1.wait_recv()
        xs2[u, 1] = (pf[u, left, 32:64, :] + xr1[u, 1].astype(F32)).astype(BF16)
        l3 = send(xs2.at[u, 1], xq.at[u, 1, hi], x_dev(-1))
        return r2, l2, r3, l3

    def reduce_third(u, copies):
        for copy in copies:
            copy.wait_recv()
        return pf[u, t] + xq[u, 0].astype(F32) + xq[u, 1].astype(F32)

    partial_sums(0, lambda n: nn(att[...], wo[:, n * 384 : n * 384 + 384]))
    p_first = reduce_first(0)

    g_further = gather_second(pair(gs), g_first)
    p_second = reduce_second(0, p_first)
    gather_third(g_further)
    for plane in range(4):
        gflat[plane] = gs[plane].astype(F32).reshape(64, D).astype(BF16)
    loads[1].wait()
    loads[3].wait()

    proj = reduce_third(0, p_second)
    mid_rows = (hs[t].astype(F32).reshape(64, D) + proj).astype(BF16)
    mid[...] = mid_rows
    x_hat2, inv_std2 = normalize(mid_rows.astype(F32))
    xhat[...] = x_hat2
    inv2[...] = inv_std2
    g2 = gain2[0:1, :]
    nb[t] = (x_hat2 * g2).astype(BF16)

    def quarter(ref):
        return lambda plane, a: ref.at[plane, pl.ds(a * 16, 16)]

    n_first = gather_first(quarter(nb), lambda a: None)

    g_all = gflat[...].reshape(256, D)
    for n in range(3):
        c = slice(n * 384, n * 384 + 384)
        ga[:, c] = nn(g_all, w2[:, c])
    n_further = gather_second(quarter(nb), n_first)
    for n in range(2):
        c = slice(n * 640, n * 640 + 640)
        gpp[:, c] = nn(g_all, perm[:, c]).astype(BF16)
    gather_third(n_further)

    root = (2.0 / np.pi) ** 0.5
    nb_all = nb[...].reshape(256, D)
    for n in range(3):
        c = slice(n * 384, n * 384 + 384)
        pre = nn(nb_all, w1[:, c])
        square = pre * pre
        th = jnp.tanh(root * (pre + 0.044715 * (square * pre)))
        half = 0.5 * (1.0 + th)
        act[:, c] = (pre * half).astype(BF16)
        slope = half + 0.5 * pre * (1.0 - th * th) * (root * (1.0 + 3 * 0.044715 * square))
        gp[:, c] = (ga[:, c] * slope).astype(BF16)
    for n in range(2):
        c = slice(n * 640, n * 640 + 640)
        nbp[:, c] = nn(nb_all, perm[:, c]).astype(BF16)

    sl, sr = fresh(), fresh()

    def swap(src, dst, i):
        return pltpu.make_async_remote_copy(
            src_ref=src, dst_ref=dst, send_sem=ssem.at[i], recv_sem=rsem.at[i], device_id=core_dev, device_id_type=MESH
        )

    @pl.when(core == 0)
    def _():
        swap(gpp, lp, sl).start()
        swap(act, rp.at[1], sr).start()
        rp[0] = gp[...]
        lt[:, 0:256] = nbp[...].T

    @pl.when(core == 1)
    def _():
        swap(nbp, lp, sl).start()
        swap(gp, rp.at[1], sr).start()
        rp[0] = act[...]
        lt[:, 0:256] = gpp[...].T

    swap_l, swap_r = swap(gpp, lp, sl), swap(act, rp.at[1], sr)
    started.extend((swap_l, swap_r))

    partial_sums(1, lambda n: nt(act[...], w2[n * 384 : n * 384 + 384, :]))
    d_first = reduce_first(1)
    partial_sums(2, lambda n: nt(gp[...], w1[n * 384 : n * 384 + 384, :]))
    e_first = reduce_first(2)
    d_second = reduce_second(1, d_first)

    swap_l.wait_recv()
    lt[:, 256:512] = lp[...].T
    swap_r.wait_recv()

    def grad_b(i, carry):
        block = lt[pl.ds(pl.multiple_of(i * 320, 320), 320), :]
        value = nn(block, rp[:, :, CA:].reshape(512, CB))
        for m in range(8):
            wb[i * 2 + m // 4, m % 4] = value[m * SLAB : (m + 1) * SLAB].astype(BF16)
        return carry

    def grad_a(i, carry):
        block = lt[pl.ds(pl.multiple_of(i * 320, 320), 320), :]
        value = nn(block, rp[:, :, :CA].reshape(512, CA))
        for m in range(8):
            wa[m % 4, i * 2 + m // 4] = value[m * SLAB : (m + 1) * SLAB].astype(BF16)
        return carry

    def add(a, b):
        return (a.astype(F32) + b.astype(F32)).astype(BF16)

    def b_first(u):
        far = wrap(zz + 4, 8)
        return [send(wb.at[far, u * 2 + d], zb1.at[u, d], z_dev(1 - 2 * d)) for d in range(2)]

    def b_step(n, u, copies):
        result = []
        for d in range(2):
            sign = 1 - 2 * d
            chunk = wrap(zz + sign * (3 - n), 8)
            copies[d].wait_recv()
            if n == 0:
                zbs[n, u, d, d] = add(wb[chunk, u * 2 + d], zb1[u, d])
                zbs[n, u, d, 1 - d] = wb[chunk, u * 2 + 1 - d]
            else:
                for i in range(2):
                    zbs[n, u, d, i] = add(wb[chunk, u * 2 + i], zbq[n - 1, u, d, i])
            result.append(send(zbs.at[n, u, d], zbq.at[n, u, d], z_dev(sign)))
        return result

    def b_last(u, copies):
        for copy in copies:
            copy.wait_recv()
        for i in range(2):
            rb[u * 2 + i] = (
                wb[zz, u * 2 + i].astype(F32) + zbq[2, u, 0, i].astype(F32) + zbq[2, u, 1, i].astype(F32)
            ).astype(BF16)

    def a_first():
        far, up, down = wrap(y + 2, 4), wrap(y + 1, 4), wrap(y - 1, 4)
        lo, hi = pl.ds(0, 4), pl.ds(4, 4)
        u1 = send(wa.at[far, lo], ya1.at[0], y_dev(1))
        d1 = send(wa.at[far, hi], ya1.at[1], y_dev(-1))
        u2 = send(wa.at[up, hi], yaq.at[0, hi], y_dev(1))
        d2 = send(wa.at[down, lo], yaq.at[1, lo], y_dev(-1))
        return u1, d1, u2, d2

    def a_second(copies):
        up, down = wrap(y + 1, 4), wrap(y - 1, 4)
        u1, d1, u2, d2 = copies
        u1.wait_recv()

        def body_up(i, carry):
            yas[0, i] = add(wa[up, i], ya1[0, i])
            return carry

        lax.fori_loop(0, 4, body_up, 0)
        u3 = send(yas.at[0], yaq.at[0, pl.ds(0, 4)], y_dev(1))
        d1.wait_recv()

        def body_down(i, carry):
            yas[1, i] = add(wa[down, i + 4], ya1[1, i])
            return carry

        lax.fori_loop(0, 4, body_down, 0)
        d3 = send(yas.at[1], yaq.at[1, pl.ds(4, 4)], y_dev(-1))
        return u2, d2, u3, d3

    def a_last(copies):
        for copy in copies:
            copy.wait_recv()

        def body(i, carry):
            ra[i] = (wa[y, i].astype(F32) + yaq[0, i].astype(F32) + yaq[1, i].astype(F32)).astype(BF16)
            return carry

        lax.fori_loop(0, 8, body, 0)

    HALF = 384

    def az_first():
        far = wrap(zz + 4, 8)
        up = send(ra.at[far, :, pl.ds(0, HALF)], za1.at[0, :, pl.ds(0, HALF)], z_dev(1))
        down = send(ra.at[far, :, pl.ds(HALF, CA - HALF)], za1.at[1, :, pl.ds(HALF, CA - HALF)], z_dev(-1))
        return [up, down]

    def az_step(n, copies):
        result = []
        for d in range(2):
            sign = 1 - 2 * d
            chunk = wrap(zz + sign * (3 - n), 8)
            copies[d].wait_recv()
            if n == 0:
                taken = slice(0, HALF) if d == 0 else slice(HALF, CA)
                other = slice(HALF, CA) if d == 0 else slice(0, HALF)
                zas[n, d, :, taken] = add(ra[chunk, :, taken], za1[d, :, taken])
                zas[n, d, :, other] = ra[chunk, :, other]
            else:
                zas[n, d] = add(ra[chunk], zaq[n - 1, d])
            result.append(send(zas.at[n, d], zaq.at[n, d], z_dev(sign)))
        return result

    def az_last(copies):
        for copy in copies:
            copy.wait_recv()
        return ra[zz].astype(F32) + zaq[2, 0].astype(F32) + zaq[2, 1].astype(F32)

    def by_first():
        far, up, down = wrap(y + 2, 4), wrap(y + 1, 4), wrap(y - 1, 4)
        lo, hi = pl.ds(0, 256), pl.ds(256, 256)
        u1 = send(rb.at[far, :, lo], yb1.at[0], y_dev(1))
        d1 = send(rb.at[far, :, hi], yb1.at[1], y_dev(-1))
        u2 = send(rb.at[up, :, hi], ybq.at[0, :, hi], y_dev(1))
        d2 = send(rb.at[down, :, lo], ybq.at[1, :, lo], y_dev(-1))
        return u1, d1, u2, d2

    def by_second(copies):
        up, down = wrap(y + 1, 4), wrap(y - 1, 4)
        u1, d1, u2, d2 = copies
        u1.wait_recv()
        ybs[0] = add(rb[up, :, 0:256], yb1[0])
        u3 = send(ybs.at[0], ybq.at[0, :, pl.ds(0, 256)], y_dev(1))
        d1.wait_recv()
        ybs[1] = add(rb[down, :, 256:512], yb1[1])
        d3 = send(ybs.at[1], ybq.at[1, :, pl.ds(256, 256)], y_dev(-1))
        return u2, d2, u3, d3

    def by_last(copies):
        for copy in copies:
            copy.wait_recv()
        return rb[y].astype(F32) + ybq[0].astype(F32) + ybq[1].astype(F32)

    lax.fori_loop(0, 4, grad_b, 0)
    b1 = [b_first(0), b_first(1)]
    lax.fori_loop(0, 4, grad_a, 0)
    a1 = a_first()
    e_second = reduce_second(2, e_first)
    b2 = [b_step(0, u, b1[u]) for u in range(2)]

    down_rows = reduce_third(1, d_second)
    bo[...] = (mid[...].astype(F32) + down_rows).reshape(8, 8, D).astype(BF16)
    exchange(lambda j, peer: bo.at[j], out_b.at[s], base_b)
    a2 = a_second(a1)
    b3 = [b_step(1, u, b2[u]) for u in range(2)]

    scaled = reduce_third(2, e_second) * g2
    x_hat2 = xhat[...]
    plain = jnp.mean(scaled, -1, keepdims=True)
    cross = jnp.mean(scaled * x_hat2, -1, keepdims=True)
    upstream = gs[t].astype(F32).reshape(64, D)
    go[...] = (upstream + inv2[...] * (scaled - plain - x_hat2 * cross)).reshape(8, 8, D).astype(BF16)
    exchange(lambda j, peer: go.at[j], out_g.at[s], base_gm)

    def out_view(ref):
        return lambda plane, a: ref.at[pl.ds(peer_seq(plane, a, 0), 2)]

    o_first = gather_first(out_view(out_b), slabs_arrived(out_b.at[s], base_b))
    b4 = [b_step(2, u, b3[u]) for u in range(2)]
    m_first = gather_first(out_view(out_g), slabs_arrived(out_g.at[s], base_gm))
    o_further = gather_second(out_view(out_b), o_first)
    a_last(a2)
    az1 = az_first()
    b_last(0, b4[0])
    b_last(1, b4[1])
    by1 = by_first()
    m_further = gather_second(out_view(out_g), m_first)
    az2 = az_step(0, az1)
    by2 = by_second(by1)
    az3 = az_step(1, az2)
    fin_b = by_last(by2)
    az4 = az_step(2, az3)
    fin_a = az_last(az4)
    for c in range(2):
        fin[c, :, 0:CA] = fin_a[c * 18 : c * 18 + 18]
        fin[c, :, CA:] = fin_b[c * 18 : c * 18 + 18]
    sf = fresh()

    @pl.when(core == 0)
    def _():
        swap(fin.at[1], out_1, sf).start()
        own = pltpu.make_async_copy(fin.at[0], out_1, asem)
        own.start()
        own.wait()
        swap(fin.at[1], out_2, sf).wait()

    @pl.when(core == 1)
    def _():
        swap(fin.at[0], out_2, sf).start()
        own = pltpu.make_async_copy(fin.at[1], out_2, asem)
        own.start()
        own.wait()
        swap(fin.at[0], out_1, sf).wait()

    gather_third(o_further)
    gather_third(m_further)

    exchange_sent(lambda j, peer: hid.at[peer], base_h)
    exchange_sent(lambda j, peer: og.at[peer], base_g)
    exchange_sent(lambda j, peer: bo.at[j], base_b)
    exchange_sent(lambda j, peer: go.at[j], base_gm)
    for copy in started:
        copy.wait_send()


def local(hidden_in, norm1_gain, qkv_weight, out_weight, norm2_gain, fc1_weight, fc2_weight, out_grad):
    anywhere = pl.BlockSpec(memory_space=pl.ANY)
    vmem = pl.BlockSpec(memory_space=pltpu.VMEM)
    shapes = [
        ((4, 8, 8, D), BF16), ((4, 8, 8, D), BF16),
        ((3 * QC, D), BF16), ((QC, D), BF16), ((D, FQ), BF16), ((D, FQ), BF16),
        ((4, 64, D), BF16), ((256, QC), BF16), ((4, 64, D), BF16), ((256, FQ), F32),
        ((256, FQ), BF16), ((256, FQ), BF16), ((4, 64, D), BF16),
        ((3, 4, 64, D), F32), ((3, 4, 64, D), BF16),
        ((3, 2, 32, D), BF16), ((3, 2, 32, D), BF16), ((3, 2, 64, D), BF16),
        ((64, D), BF16), ((64, D), F32), ((64, 1), F32), ((8, 8, D), BF16), ((8, 8, D), BF16),
        ((D, ROWS), BF16), ((256, ROWS), BF16), ((256, ROWS), BF16),
        ((256, ROWS), BF16), ((2, 256, FQ), BF16), ((ROWS, 512), BF16),
        ((4, 8, SLAB, CA), BF16), ((2, 4, SLAB, CA), BF16), ((2, 4, SLAB, CA), BF16), ((2, 8, SLAB, CA), BF16),
        ((8, SLAB, CA), BF16), ((2, SLAB, CA), BF16), ((3, 2, SLAB, CA), BF16), ((3, 2, SLAB, CA), BF16),
        ((8, 4, SLAB, CB), BF16), ((2, 2, SLAB, CB), BF16), ((3, 2, 2, 2, SLAB, CB), BF16), ((3, 2, 2, 2, SLAB, CB), BF16),
        ((4, SLAB, CB), BF16), ((2, SLAB, 256), BF16), ((2, SLAB, 256), BF16), ((2, SLAB, CB), BF16),
        ((2, 18, FQ), F32),
    ]
    scratch = [pltpu.VMEM(shape, kind) for shape, kind in shapes]
    scratch += [
        pltpu.SemaphoreType.DMA((N_SEM,)), pltpu.SemaphoreType.DMA((N_SEM,)),
        pltpu.SemaphoreType.DMA((4,)), pltpu.SemaphoreType.DMA,
    ]
    rows = lambda gain: jnp.broadcast_to(gain.reshape(1, D), (8, D))
    block, grad_mid, grad_fc1, grad_fc2 = pl.pallas_call(
        kernel,
        out_shape=[
            jax.ShapeDtypeStruct((32, 8, D), BF16),
            jax.ShapeDtypeStruct((32, 8, D), BF16),
            jax.ShapeDtypeStruct((18, FQ), F32),
            jax.ShapeDtypeStruct((18, FQ), F32),
        ],
        in_specs=[anywhere, vmem, anywhere, anywhere, vmem, anywhere, anywhere, anywhere, vmem],
        out_specs=[anywhere] * 4,
        scratch_shapes=scratch,
        compiler_params=pltpu.CompilerParams(
            collective_id=0, has_side_effects=True, vmem_limit_bytes=60 * 1024 * 1024
        ),
    )(
        hidden_in.reshape(32, 8, D),
        rows(norm1_gain),
        qkv_weight.transpose(1, 2, 0).reshape(3 * QC, D),
        out_weight,
        rows(norm2_gain),
        fc1_weight,
        fc2_weight,
        out_grad.reshape(32, 8, D),
        jnp.asarray(slab_sources()),
    )
    shape = hidden_in.shape
    return block.reshape(shape), grad_mid.reshape(shape), grad_fc1, grad_fc2


def solution(mesh):
    return jax.shard_map(
        local,
        mesh=mesh,
        in_specs=(
            P("dp", "seq", None, None),
            P(),
            P(None, None, "tensor"),
            P("tensor", None),
            P(),
            P(None, "tensor"),
            P(None, "tensor"),
            P("dp", "seq", None, None),
        ),
        out_specs=(
            P("dp", "seq", None, None),
            P("dp", "seq", None, None),
            P(("seq", "dp"), "tensor"),
            P(("seq", "dp"), "tensor"),
        ),
        check_vma=False,
    )
```

time: 403 us -> 109 us (0.27)
  waiting for transfers between devices: 244 us -> 0 us
  Pallas kernels: 0 us -> 98.9 us
  blocking collectives: 85.4 us -> 0 us
  matrix products: 24.2 us -> 0 us
  other arithmetic: 15.7 us -> 0 us
  between operations: 14.6 us -> 0.65 us
  local copies, waits for them, and re-layouts: 17.5 us -> 8.71 us
    unnamed x5 -> x0, waiting for transfers between devices: 190 us -> none
    pallas_call x0 -> x1, Pallas kernels: none -> 98.9 us  [local(): pl.pallas_call(kernel, out_shape=[jax.ShapeDtypeStruct((32, 8, D), BF16),...]
    reduce_scatter x3 -> x0, waiting for transfers between devices: 54.3 us -> none  [the longest x1 27.8 us: local(): lax.psum_scatter(contract_last(act, fc2_weight), 'tensor', scatter_dimens...]
    all_to_all x2 -> x0, blocking collectives: 52.6 us -> none  [the longest x1 35.3 us: local(): block = lax.all_to_all(qkv, 'seq', split_axis=2, concat_axis=1, tiled=True)]
    all_gather x3 -> x0, blocking collectives: 32.8 us -> none  [the longest x1 11.3 us: local(): lax.all_gather(grad_mid_share, 'tensor', axis=0, tiled=True)]
    dot_general x9 -> x0, matrix products: 22.8 us -> none  [the longest x2 8.01 us: contract_first(): lax.dot_general(left, right, (((0,), (0,)), ((), ())), preferred_element_...]
    concatenate x1 -> x0, other arithmetic: 9.01 us -> none  [local(): jnp.concatenate([contract_first(norm_b, grad_pre), contract_first(grad_fl...]
    reduce_sum x5 -> x0, other arithmetic: 5.27 us -> none  [the longest x2 2.51 us: normalize(): center = values - jnp.mean(values, -1, keepdims=True)]
  transfers between devices with their start and end apart: 4 -> 0, of which waited for: 4 -> 0; matrix products, arithmetic and copies ran while one was open for 6% -> 0% of each run, Pallas kernels for 0% -> 0%
where the time goes in v1:
time: 109 us; the launch traced here: 108 us
  Pallas kernels  98.9 us (91%)
  local copies, waits for them, and re-layouts  8.71 us (8%)
    pallas_call x1, Pallas kernels, local(): pl.pallas_call(kernel, out_shape=[jax.ShapeDtypeStruct((32, 8, D), BF16),...  98.9 us
    unnamed x6, local copies, waits for them, and re-layouts  6.08 us
    broadcast_in_dim x2, local copies, waits for them, and re-layouts, local(): rows = lambda gain: jnp.broadcast_to(gain.reshape(1, D), (8, D))  2.63 us

profile of v1, /device:TPU:1, one launch (start us, length us, event | category | flops | bytes accessed | tf_op | source)
XLA Modules:
  0.0 108.3 jit_solution(2714873247819691331)
XLA Ops:
  0.6 1.3 %broadcast_in_dim.4.gain1 = f32[8,1152]{1,0:T(8,128)} broadcast(f32[1152]{0:T(1024)} %param.10), dimensions={1} | broadcast | bytes 41472 | tf_op jit(solution)/shard_map/broadcast_in_dim | solution.py:586
  1.9 1.3 %broadcast_in_dim.5.gain2 = f32[8,1152]{1,0:T(8,128)} broadcast(f32[1152]{0:T(1024)} %param.13), dimensions={1} | broadcast | bytes 41472 | tf_op jit(solution)/shard_map/broadcast_in_dim | solution.py:586
  3.3 98.9 %shard_map.120 = (bf16[32,8,1152]{2,1,0:T(8,128)(2,1)}, bf16[32,8,1152]{2,1,0:T(8,128)(2,1)}, f32[18,1152]{1,0:T(8,128)}, f32[18,1152]{1,0:T(8,128)}) custom-call(bf16[32,8,1152]{2,1,0:T(8,128)(2,1)} %bitcast.8, f32[8,1152]{1,0:T(8,128)} %broadcast_in_dim.4.gain1, bf16[864,1152]{1,0:T(8,128)(2,1)} %bitcast.7, bf16[288,1152]{1,0:T(8,128)(2,1)} %wo_h.1, ...), custom_call_target="tpu_custom_call" | custom-call | tf_op jit(solution)/shard_map/pallas_call | solution.py:587
  102.2 0.0 copy-start
  102.2 2.0 %copy.17 = bf16[1,1,256,1152]{3,2,1,0:T(8,128)(2,1)} copy(bf16[1,1,256,1152]{3,2,1,0:T(8,128)(2,1)} %bitcast.11) | data formatting | bytes 1179648
  104.2 1.9 %copy.18 = bf16[1,1,256,1152]{3,2,1,0:T(8,128)(2,1)} copy(bf16[1,1,256,1152]{3,2,1,0:T(8,128)(2,1)} %bitcast.10) | data formatting | bytes 1179648
  106.1 1.5 %copy.19 = f32[18,1152]{1,0:T(8,128)} copy(f32[18,1152]{1,0:T(8,128)} %get-tuple-element.18) | data formatting | bytes 165888
  107.6 0.0 copy-done
  107.7 0.6 copy.20
Async XLA Ops:
  102.2 5.4 %copy-start = (f32[18,1152]{1,0:T(8,128)S(1)}, f32[18,1152]{1,0:T(8,128)}, u32[]{:S(2)}) copy-start(f32[18,1152]{1,0:T(8,128)} %get-tuple-element.19) | copy-start | bytes 248836

commit v2 on v1

--- a/solution.py
+++ b/solution.py
@@ -24,14 +24,14 @@
 N_SEM = 160
 
 
-def slab_sources():
-    source = np.full((8, 4, SLAB), -1, np.int32)
-    for z in range(8):
-        for y in range(4):
-            for core in range(2):
-                first = ((z // 2) * 8 + y * 2 + core) * 36 + (z % 2) * 18
-                source[z, y, core * 18 : core * 18 + 18] = np.arange(first, first + 18)
-    return np.broadcast_to(source.reshape(1, ROWS), (8, ROWS)).copy()
+def slab_sources(first, count):
+    n = lax.broadcasted_iota(jnp.int32, (count, 1), 0) + first
+    slab = (n * 1639) >> 16
+    within = n - slab * SLAB
+    core = jnp.where(within >= 18, 1, 0)
+    z, y = slab >> 2, slab & 3
+    source = (((z >> 1) * 4 + y) * 2 + core) * 36 + (z & 1) * 18 + within - core * 18
+    return jnp.where(within < 36, source, -1)
 
 
 def nn(a, b):
@@ -49,14 +49,14 @@
 
 
 def kernel(
-    hid, gain1, wq_h, wo_h, gain2, w1_h, w2_h, og, idx,
+    hid, gain1, wq_h, wo_h, gain2, w1_h, w2_h, og,
     out_b, out_g, out_1, out_2,
-    hs, gs, wq, wo, w1, w2, na, att, gflat, ga, act, gp, nb,
-    pf, pb, xr1, xs2, xq, mid, xhat, inv2, bo, go,
-    perm, nbp, gpp, lp, rp, lt,
+    hs, gs, wq, wo, w1, w2, na, att, gflat, ga, nb,
+    pf, pb, xr1, xs2, xq, ms, mr, xhat, inv2, bo, go,
+    perm, lbuf, rbuf,
     wa, ya1, yas, yaq, ra, za1, zas, zaq,
     wb, zb1, zbs, zbq, rb, yb1, ybs, ybq, fin,
-    ssem, rsem, lsem, asem,
+    ssem, rsem, lsem, gsem, osem, asem,
 ):
     t = lax.axis_index("tensor")
     s = lax.axis_index("seq")
@@ -150,18 +150,26 @@
                 def _():
                     pltpu.make_async_copy(src, src, ssem.at[base + j]).wait()
 
-    base_h, base_g, base_b, base_gm = fresh(8), fresh(8), fresh(8), fresh(8)
+    base_h, base_m = fresh(8), fresh(8)
     here = hs.at[t, zh * 2 + core]
     exchange(lambda j, peer: hid.at[peer], here, base_h)
-    exchange(lambda j, peer: og.at[peer], gs.at[t, zh * 2 + core], base_g)
-
-    def gather_first(view, arrived):
+
+    turned = [
+        pltpu.make_async_copy(
+            og.at[pl.ds(peer_seq(plane, a, 0), 2)], gs.at[plane, pl.ds(a * 2, 2)], gsem.at[plane * 4 + a]
+        )
+        for plane in range(4)
+        for a in range(4)
+    ]
+    for copy in turned:
+        copy.start()
+
+    def gather_first(view, arrived, own=None):
         copies = []
         for a in range(4):
             arrived(a)
-            copies.append(
-                (send(view(t, a), view(t, a), x_dev(1)), send(view(t, a), view(t, a), x_dev(-1)))
-            )
+            src = view(t, a) if own is None else own(a)
+            copies.append((send(src, view(t, a), x_dev(1)), send(src, view(t, a), x_dev(-1))))
         return copies
 
     def gather_second(view, copies):
@@ -193,13 +201,15 @@
 
     def make_perm(i, carry):
         first = pl.multiple_of(i * 128, 128)
-        row = lax.broadcasted_iota(jnp.int32, (128, ROWS), 0) + first
-        perm[pl.ds(first, 128), :] = jnp.where(row == idx[0:1, :], 1.0, 0.0).astype(BF16)
+        wanted = slab_sources(first, 128)
+        perm[pl.ds(first, 128), :] = jnp.where(
+            lax.broadcasted_iota(jnp.int32, (128, D), 1) == wanted, 1.0, 0.0
+        ).astype(BF16)
         return carry
 
-    lax.fori_loop(0, 9, make_perm, 0)
-
-    g1 = gain1[0:1, :]
+    lax.fori_loop(0, ROWS // 128, make_perm, 0)
+
+    g1 = gain1[...].reshape(1, D)
 
     def norm_share(plane):
         x_hat, _ = normalize(hs[plane].astype(F32).reshape(64, D))
@@ -210,7 +220,6 @@
     h_further = gather_second(pair(hs), h_first)
     norm_share(wrap(t - 1, 4))
     norm_share(wrap(t + 1, 4))
-    g_first = gather_first(pair(gs), slabs_arrived(here, base_g))
     gather_third(h_further)
     norm_share(wrap(t + 2, 4))
 
@@ -268,97 +277,82 @@
     partial_sums(0, lambda n: nn(att[...], wo[:, n * 384 : n * 384 + 384]))
     p_first = reduce_first(0)
 
-    g_further = gather_second(pair(gs), g_first)
     p_second = reduce_second(0, p_first)
-    gather_third(g_further)
+
+    for copy in turned:
+        copy.wait()
     for plane in range(4):
         gflat[plane] = gs[plane].astype(F32).reshape(64, D).astype(BF16)
     loads[1].wait()
     loads[3].wait()
 
     proj = reduce_third(0, p_second)
-    mid_rows = (hs[t].astype(F32).reshape(64, D) + proj).astype(BF16)
-    mid[...] = mid_rows
-    x_hat2, inv_std2 = normalize(mid_rows.astype(F32))
-    xhat[...] = x_hat2
-    inv2[...] = inv_std2
-    g2 = gain2[0:1, :]
-    nb[t] = (x_hat2 * g2).astype(BF16)
-
-    def quarter(ref):
-        return lambda plane, a: ref.at[plane, pl.ds(a * 16, 16)]
-
-    n_first = gather_first(quarter(nb), lambda a: None)
-
+    ms[...] = (hs[t].astype(F32).reshape(64, D) + proj).reshape(8, 8, D).astype(BF16)
+    back = mr.at[zh * 2 + core]
+    exchange(lambda j, peer: ms.at[j], back, base_m)
     g_all = gflat[...].reshape(256, D)
     for n in range(3):
         c = slice(n * 384, n * 384 + 384)
         ga[:, c] = nn(g_all, w2[:, c])
-    n_further = gather_second(quarter(nb), n_first)
+    for j in range(8):
+        exchange_arrived(back, base_m, j)
+
+    mid_rows = mr[...].astype(F32).reshape(64, D)
+    x_hat2, inv_std2 = normalize(mid_rows)
+    xhat[...] = x_hat2
+    inv2[...] = inv_std2
+    g2 = gain2[...].reshape(1, D)
+    nb[t] = (x_hat2 * g2).astype(BF16)
+
+    def quarter(ref):
+        return lambda plane, a: ref.at[plane, pl.ds(a * 16, 16)]
+
+    n_first = gather_first(quarter(nb), lambda a: None)
+
     for n in range(2):
         c = slice(n * 640, n * 640 + 640)
-        gpp[:, c] = nn(g_all, perm[:, c]).astype(BF16)
+        lbuf[0, c, :] = nt(perm[c, :], g_all).astype(BF16)
+    n_further = gather_second(quarter(nb), n_first)
     gather_third(n_further)
+    nb_all = nb[...].reshape(256, D)
+    for n in range(2):
+        c = slice(n * 640, n * 640 + 640)
+        lbuf[1, c, :] = nt(perm[c, :], nb_all).astype(BF16)
+
+    swapped = [send(lbuf.at[core], lbuf.at[2], core_dev)]
+    kept = 1 - core
 
     root = (2.0 / np.pi) ** 0.5
-    nb_all = nb[...].reshape(256, D)
     for n in range(3):
         c = slice(n * 384, n * 384 + 384)
         pre = nn(nb_all, w1[:, c])
         square = pre * pre
         th = jnp.tanh(root * (pre + 0.044715 * (square * pre)))
         half = 0.5 * (1.0 + th)
-        act[:, c] = (pre * half).astype(BF16)
+        rbuf[0, :, c] = (pre * half).astype(BF16)
         slope = half + 0.5 * pre * (1.0 - th * th) * (root * (1.0 + 3 * 0.044715 * square))
-        gp[:, c] = (ga[:, c] * slope).astype(BF16)
-    for n in range(2):
-        c = slice(n * 640, n * 640 + 640)
-        nbp[:, c] = nn(nb_all, perm[:, c]).astype(BF16)
-
-    sl, sr = fresh(), fresh()
-
-    def swap(src, dst, i):
-        return pltpu.make_async_remote_copy(
-            src_ref=src, dst_ref=dst, send_sem=ssem.at[i], recv_sem=rsem.at[i], device_id=core_dev, device_id_type=MESH
-        )
-
-    @pl.when(core == 0)
-    def _():
-        swap(gpp, lp, sl).start()
-        swap(act, rp.at[1], sr).start()
-        rp[0] = gp[...]
-        lt[:, 0:256] = nbp[...].T
-
-    @pl.when(core == 1)
-    def _():
-        swap(nbp, lp, sl).start()
-        swap(gp, rp.at[1], sr).start()
-        rp[0] = act[...]
-        lt[:, 0:256] = gpp[...].T
-
-    swap_l, swap_r = swap(gpp, lp, sl), swap(act, rp.at[1], sr)
-    started.extend((swap_l, swap_r))
-
-    partial_sums(1, lambda n: nt(act[...], w2[n * 384 : n * 384 + 384, :]))
+        rbuf[1, :, c] = (ga[:, c] * slope).astype(BF16)
+        part = pl.ds(n * 384, 384)
+        swapped.append(send(rbuf.at[core, :, part], rbuf.at[2, :, part], core_dev))
+
+    partial_sums(1, lambda n: nt(rbuf[0], w2[n * 384 : n * 384 + 384, :]))
     d_first = reduce_first(1)
-    partial_sums(2, lambda n: nt(gp[...], w1[n * 384 : n * 384 + 384, :]))
+    partial_sums(2, lambda n: nt(rbuf[1], w1[n * 384 : n * 384 + 384, :]))
     e_first = reduce_first(2)
     d_second = reduce_second(1, d_first)
-
-    swap_l.wait_recv()
-    lt[:, 256:512] = lp[...].T
-    swap_r.wait_recv()
+    for copy in swapped:
+        copy.wait_recv()
 
     def grad_b(i, carry):
-        block = lt[pl.ds(pl.multiple_of(i * 320, 320), 320), :]
-        value = nn(block, rp[:, :, CA:].reshape(512, CB))
+        rows = pl.ds(pl.multiple_of(i * 320, 320), 320)
+        value = nn(lbuf[kept, rows, :], rbuf[kept, :, CA:]) + nn(lbuf[2, rows, :], rbuf[2, :, CA:])
         for m in range(8):
             wb[i * 2 + m // 4, m % 4] = value[m * SLAB : (m + 1) * SLAB].astype(BF16)
         return carry
 
     def grad_a(i, carry):
-        block = lt[pl.ds(pl.multiple_of(i * 320, 320), 320), :]
-        value = nn(block, rp[:, :, :CA].reshape(512, CA))
+        rows = pl.ds(pl.multiple_of(i * 320, 320), 320)
+        value = nn(lbuf[kept, rows, :], rbuf[kept, :, :CA]) + nn(lbuf[2, rows, :], rbuf[2, :, :CA])
         for m in range(8):
             wa[m % 4, i * 2 + m // 4] = value[m * SLAB : (m + 1) * SLAB].astype(BF16)
         return carry
@@ -494,9 +488,20 @@
     e_second = reduce_second(2, e_first)
     b2 = [b_step(0, u, b1[u]) for u in range(2)]
 
+    def out_view(ref):
+        return lambda plane, a: ref.at[pl.ds(peer_seq(plane, a, 0), 2)]
+
+    def give(rows, ref, base):
+        for a in range(4):
+            copy = pltpu.make_async_copy(rows.at[pl.ds(a * 2, 2)], out_view(ref)(t, a), osem.at[base + a])
+            copy.start()
+            placed.append(copy)
+        return gather_first(out_view(ref), lambda a: None, lambda a: rows.at[pl.ds(a * 2, 2)])
+
+    placed = []
     down_rows = reduce_third(1, d_second)
-    bo[...] = (mid[...].astype(F32) + down_rows).reshape(8, 8, D).astype(BF16)
-    exchange(lambda j, peer: bo.at[j], out_b.at[s], base_b)
+    bo[...] = (mr[...].astype(F32).reshape(64, D) + down_rows).reshape(8, 8, D).astype(BF16)
+    o_first = give(bo, out_b, 0)
     a2 = a_second(a1)
     b3 = [b_step(1, u, b2[u]) for u in range(2)]
 
@@ -506,23 +511,18 @@
     cross = jnp.mean(scaled * x_hat2, -1, keepdims=True)
     upstream = gs[t].astype(F32).reshape(64, D)
     go[...] = (upstream + inv2[...] * (scaled - plain - x_hat2 * cross)).reshape(8, 8, D).astype(BF16)
-    exchange(lambda j, peer: go.at[j], out_g.at[s], base_gm)
-
-    def out_view(ref):
-        return lambda plane, a: ref.at[pl.ds(peer_seq(plane, a, 0), 2)]
-
-    o_first = gather_first(out_view(out_b), slabs_arrived(out_b.at[s], base_b))
+    m_first = give(go, out_g, 4)
+
     b4 = [b_step(2, u, b3[u]) for u in range(2)]
-    m_first = gather_first(out_view(out_g), slabs_arrived(out_g.at[s], base_gm))
-    o_further = gather_second(out_view(out_b), o_first)
     a_last(a2)
     az1 = az_first()
     b_last(0, b4[0])
     b_last(1, b4[1])
     by1 = by_first()
-    m_further = gather_second(out_view(out_g), m_first)
+    o_further = gather_second(out_view(out_b), o_first)
     az2 = az_step(0, az1)
     by2 = by_second(by1)
+    m_further = gather_second(out_view(out_g), m_first)
     az3 = az_step(1, az2)
     fin_b = by_last(by2)
     az4 = az_step(2, az3)
@@ -532,31 +532,50 @@
         fin[c, :, CA:] = fin_b[c * 18 : c * 18 + 18]
     sf = fresh()
 
+    def hand_over(src, dst):
+        return pltpu.make_async_remote_copy(
+            src_ref=src, dst_ref=dst, send_sem=ssem.at[sf], recv_sem=rsem.at[sf], device_id=core_dev, device_id_type=MESH
+        )
+
     @pl.when(core == 0)
     def _():
-        swap(fin.at[1], out_1, sf).start()
+        hand_over(fin.at[1], out_1).start()
         own = pltpu.make_async_copy(fin.at[0], out_1, asem)
         own.start()
         own.wait()
-        swap(fin.at[1], out_2, sf).wait()
+        hand_over(fin.at[1], out_2).wait()
 
     @pl.when(core == 1)
     def _():
-        swap(fin.at[0], out_2, sf).start()
+        hand_over(fin.at[0], out_2).start()
         own = pltpu.make_async_copy(fin.at[1], out_2, asem)
         own.start()
         own.wait()
-        swap(fin.at[0], out_1, sf).wait()
+        hand_over(fin.at[0], out_1).wait()
 
     gather_third(o_further)
     gather_third(m_further)
+    for copy in placed:
+        copy.wait()
 
     exchange_sent(lambda j, peer: hid.at[peer], base_h)
-    exchange_sent(lambda j, peer: og.at[peer], base_g)
-    exchange_sent(lambda j, peer: bo.at[j], base_b)
-    exchange_sent(lambda j, peer: go.at[j], base_gm)
+    exchange_sent(lambda j, peer: ms.at[j], base_m)
     for copy in started:
         copy.wait_send()
+
+
+def place(*refs):
+    sources, results, sems = refs[:4], refs[4:8], refs[8]
+    copies = []
+    for src, dst, parts in zip(sources, results, (4, 4, 1, 1)):
+        step = src.shape[0] // parts
+        for i in range(parts):
+            rows = pl.ds(i * step, step)
+            copies.append(pltpu.make_async_copy(src.at[rows], dst.at[rows], sems.at[len(copies)]))
+    for copy in copies:
+        copy.start()
+    for copy in copies:
+        copy.wait()
 
 
 def local(hidden_in, norm1_gain, qkv_weight, out_weight, norm2_gain, fc1_weight, fc2_weight, out_grad):
@@ -565,13 +584,11 @@
     shapes = [
         ((4, 8, 8, D), BF16), ((4, 8, 8, D), BF16),
         ((3 * QC, D), BF16), ((QC, D), BF16), ((D, FQ), BF16), ((D, FQ), BF16),
-        ((4, 64, D), BF16), ((256, QC), BF16), ((4, 64, D), BF16), ((256, FQ), F32),
-        ((256, FQ), BF16), ((256, FQ), BF16), ((4, 64, D), BF16),
+        ((4, 64, D), BF16), ((256, QC), BF16), ((4, 64, D), BF16), ((256, FQ), F32), ((4, 64, D), BF16),
         ((3, 4, 64, D), F32), ((3, 4, 64, D), BF16),
         ((3, 2, 32, D), BF16), ((3, 2, 32, D), BF16), ((3, 2, 64, D), BF16),
-        ((64, D), BF16), ((64, D), F32), ((64, 1), F32), ((8, 8, D), BF16), ((8, 8, D), BF16),
-        ((D, ROWS), BF16), ((256, ROWS), BF16), ((256, ROWS), BF16),
-        ((256, ROWS), BF16), ((2, 256, FQ), BF16), ((ROWS, 512), BF16),
+        ((8, 8, D), BF16), ((8, 8, D), BF16), ((64, D), F32), ((64, 1), F32), ((8, 8, D), BF16), ((8, 8, D), BF16),
+        ((ROWS, D), BF16), ((3, ROWS, 256), BF16), ((3, 256, FQ), BF16),
         ((4, 8, SLAB, CA), BF16), ((2, 4, SLAB, CA), BF16), ((2, 4, SLAB, CA), BF16), ((2, 8, SLAB, CA), BF16),
         ((8, SLAB, CA), BF16), ((2, SLAB, CA), BF16), ((3, 2, SLAB, CA), BF16), ((3, 2, SLAB, CA), BF16),
         ((8, 4, SLAB, CB), BF16), ((2, 2, SLAB, CB), BF16), ((3, 2, 2, 2, SLAB, CB), BF16), ((3, 2, 2, 2, SLAB, CB), BF16),
@@ -581,18 +598,19 @@
     scratch = [pltpu.VMEM(shape, kind) for shape, kind in shapes]
     scratch += [
         pltpu.SemaphoreType.DMA((N_SEM,)), pltpu.SemaphoreType.DMA((N_SEM,)),
-        pltpu.SemaphoreType.DMA((4,)), pltpu.SemaphoreType.DMA,
+        pltpu.SemaphoreType.DMA((4,)), pltpu.SemaphoreType.DMA((16,)), pltpu.SemaphoreType.DMA((8,)),
+        pltpu.SemaphoreType.DMA,
     ]
-    rows = lambda gain: jnp.broadcast_to(gain.reshape(1, D), (8, D))
-    block, grad_mid, grad_fc1, grad_fc2 = pl.pallas_call(
+    results = [
+        jax.ShapeDtypeStruct((32, 8, D), BF16),
+        jax.ShapeDtypeStruct((32, 8, D), BF16),
+        jax.ShapeDtypeStruct((18, FQ), F32),
+        jax.ShapeDtypeStruct((18, FQ), F32),
+    ]
+    made = pl.pallas_call(
         kernel,
-        out_shape=[
-            jax.ShapeDtypeStruct((32, 8, D), BF16),
-            jax.ShapeDtypeStruct((32, 8, D), BF16),
-            jax.ShapeDtypeStruct((18, FQ), F32),
-            jax.ShapeDtypeStruct((18, FQ), F32),
-        ],
-        in_specs=[anywhere, vmem, anywhere, anywhere, vmem, anywhere, anywhere, anywhere, vmem],
+        out_shape=results,
+        in_specs=[anywhere, vmem, anywhere, anywhere, vmem, anywhere, anywhere, anywhere],
         out_specs=[anywhere] * 4,
         scratch_shapes=scratch,
         compiler_params=pltpu.CompilerParams(
@@ -600,15 +618,22 @@
         ),
     )(
         hidden_in.reshape(32, 8, D),
-        rows(norm1_gain),
+        norm1_gain,
         qkv_weight.transpose(1, 2, 0).reshape(3 * QC, D),
         out_weight,
-        rows(norm2_gain),
+        norm2_gain,
         fc1_weight,
         fc2_weight,
         out_grad.reshape(32, 8, D),
-        jnp.asarray(slab_sources()),
     )
+    block, grad_mid, grad_fc1, grad_fc2 = pl.pallas_call(
+        place,
+        out_shape=results,
+        in_specs=[anywhere] * 4,
+        out_specs=[anywhere] * 4,
+        scratch_shapes=[pltpu.SemaphoreType.DMA((10,))],
+        compiler_params=pltpu.CompilerParams(vmem_limit_bytes=60 * 1024 * 1024),
+    )(*made)
     shape = hidden_in.shape
     return block.reshape(shape), grad_mid.reshape(shape), grad_fc1, grad_fc2
 

time: 109 us -> 143 us (1.31)
  Pallas kernels: 98.9 us -> 142 us
  local copies, waits for them, and re-layouts: 8.71 us -> 0 us
    pallas_call x1 -> x2, Pallas kernels: 98.9 us -> 142 us  [the longest x1 98.7 us: local(): pl.pallas_call(kernel, out_shape=results, in_specs=[anywhere, vmem, anywh...]
    unnamed x6 -> x0, local copies, waits for them, and re-layouts: 6.08 us -> none
    broadcast_in_dim x2 -> x0, local copies, waits for them, and re-layouts: 2.63 us -> none  [local(): rows = lambda gain: jnp.broadcast_to(gain.reshape(1, D), (8, D))]
where the time goes in v2:
time: 143 us
  Pallas kernels  142 us (99%)
    pallas_call x1, Pallas kernels, local(): pl.pallas_call(kernel, out_shape=results, in_specs=[anywhere, vmem, anywh...  98.7 us
    pallas_call x1, Pallas kernels, local(): pl.pallas_call(place, out_shape=results, in_specs=[anywhere] * 4, out_spe...  43.6 us

profile of v2, /device:TPU:1, one launch (start us, length us, event | category | flops | bytes accessed | tf_op | source)
XLA Modules:
  0.0 143.1 jit_solution(15156481526598303569)
XLA Ops:
  0.6 98.7 %shard_map.111 = (bf16[32,8,1152]{2,1,0:T(8,128)(2,1)}, bf16[32,8,1152]{2,1,0:T(8,128)(2,1)}, f32[18,1152]{1,0:T(8,128)}, f32[18,1152]{1,0:T(8,128)}) custom-call(bf16[32,8,1152]{2,1,0:T(8,128)(2,1)} %bitcast.8, f32[1152]{0:T(1024)} %gain1.1, bf16[864,1152]{1,0:T(8,128)(2,1)} %bitcast.7, bf16[288,1152]{1,0:T(8,128)(2,1)} %wo_h.1, f32[1152]{0:T(1024)} %gain2.1, ...), custom_call_target="tpu_custom_call" | custom-call | tf_op jit(solution)/shard_map/pallas_call | solution.py:610
  99.4 43.6 %shard_map.112 = (bf16[32,8,1152]{2,1,0:T(8,128)(2,1)}, bf16[32,8,1152]{2,1,0:T(8,128)(2,1)}, f32[18,1152]{1,0:T(8,128)}, f32[18,1152]{1,0:T(8,128)}) custom-call(bf16[32,8,1152]{2,1,0:T(8,128)(2,1)} %get-tuple-element.12.refs_0_, bf16[32,8,1152]{2,1,0:T(8,128)(2,1)} %get-tuple-element.13.refs_1_, f32[18,1152]{1,0:T(8,128)} %get-tuple-element.14.refs_2_, ...), custom_call_target="tpu_custom_call" | custom-call | tf_op jit(solution)/shard_map/pallas_call | solution.py:629

commit v3 on v2

--- a/solution.py
+++ b/solution.py
@@ -18,10 +18,10 @@
 QC = 288
 SLAB = 40
 ROWS = 32 * SLAB
-CA = 640
-CB = 512
+CA = 512
+CB = 640
 EPS = 1e-06
-N_SEM = 160
+N_SEM = 200
 
 
 def slab_sources(first, count):
@@ -51,11 +51,11 @@
 def kernel(
     hid, gain1, wq_h, wo_h, gain2, w1_h, w2_h, og,
     out_b, out_g, out_1, out_2,
-    hs, gs, wq, wo, w1, w2, na, att, gflat, ga, nb,
-    pf, pb, xr1, xs2, xq, ms, mr, xhat, inv2, bo, go,
+    hs, gs, hres, wq, wo, w1, w2, na, att, arec, gflat, ga, nb,
+    pf, pb, xr1, xs2, xq, mid, xhat, inv2, bo, go,
     perm, lbuf, rbuf,
-    wa, ya1, yas, yaq, ra, za1, zas, zaq,
-    wb, zb1, zbs, zbq, rb, yb1, ybs, ybq, fin,
+    wa, ya1, yas, yaq, ra, raq,
+    wb, zb1, zbs, zbq, rb, rbq, fin,
     ssem, rsem, lsem, gsem, osem, asem,
 ):
     t = lax.axis_index("tensor")
@@ -85,21 +85,25 @@
         return a * 8 + wrap(plane - zh - y - a, 4) * 2 + k
 
     barrier = pltpu.get_barrier_semaphore()
-    for dev in (x_dev(1), x_dev(-1), y_dev(1), y_dev(-1), z_dev(1), z_dev(-1), core_dev):
+    for dev in (x_dev(1), x_dev(-1), core_dev):
         pl.semaphore_signal(barrier, inc=1, device_id=dev, device_id_type=MESH)
-    for a in range(4):
-        for k in range(2):
-            peer = peer_seq(t, a, k)
-
-            pl.semaphore_signal(barrier, inc=1, device_id={"seq": peer}, device_id_type=MESH)
+    for step in range(1, 4):
+        pl.semaphore_signal(barrier, inc=1, device_id=y_dev(step), device_id_type=MESH)
+    for step in range(1, 8):
+        pl.semaphore_signal(barrier, inc=1, device_id=z_dev(step), device_id_type=MESH)
+    for plane in range(4):
+        for a in range(4):
+            for k in range(2):
+                dev = {"seq": peer_seq(t, a, k), "tensor": plane}
+                pl.semaphore_signal(barrier, inc=1, device_id=dev, device_id_type=MESH)
 
     loads = [
         pltpu.make_async_copy(src, dst, lsem.at[i])
-        for i, (src, dst) in enumerate(((wq_h, wq), (w2_h, w2), (wo_h, wo), (w1_h, w1)))
+        for i, (src, dst) in enumerate(((wo_h, wo.at[t]), (wq_h, wq), (w2_h, w2), (w1_h, w1)))
     ]
     for load in loads:
         load.start()
-    pl.semaphore_wait(barrier, 15)
+    pl.semaphore_wait(barrier, 45)
 
     count = [0]
     started = []
@@ -150,7 +154,7 @@
                 def _():
                     pltpu.make_async_copy(src, src, ssem.at[base + j]).wait()
 
-    base_h, base_m = fresh(8), fresh(8)
+    base_h, base_m = fresh(8), fresh(32)
     here = hs.at[t, zh * 2 + core]
     exchange(lambda j, peer: hid.at[peer], here, base_h)
 
@@ -159,6 +163,9 @@
             og.at[pl.ds(peer_seq(plane, a, 0), 2)], gs.at[plane, pl.ds(a * 2, 2)], gsem.at[plane * 4 + a]
         )
         for plane in range(4)
+        for a in range(4)
+    ] + [
+        pltpu.make_async_copy(hid.at[pl.ds(peer_seq(t, a, 0), 2)], hres.at[pl.ds(a * 2, 2)], gsem.at[16 + a])
         for a in range(4)
     ]
     for copy in turned:
@@ -199,6 +206,16 @@
 
         return arrived
 
+    def wo_part(plane, first, size):
+        return wo.at[plane, pl.ds(pl.multiple_of(core * 144 + first, 16), size)]
+
+    def wo_send(first, size):
+        src = wo_part(t, first, size)
+        return send(src, src, x_dev(1)), send(src, src, x_dev(-1))
+
+    loads[0].wait()
+    wo_first = [wo_send(0, 48)]
+
     def make_perm(i, carry):
         first = pl.multiple_of(i * 128, 128)
         wanted = slab_sources(first, 128)
@@ -218,16 +235,26 @@
     h_first = gather_first(pair(hs), slabs_arrived(here, base_h))
     norm_share(t)
     h_further = gather_second(pair(hs), h_first)
+    wo_first.append(wo_send(48, 96))
     norm_share(wrap(t - 1, 4))
     norm_share(wrap(t + 1, 4))
     gather_third(h_further)
     norm_share(wrap(t + 2, 4))
 
-    loads[0].wait()
+    loads[1].wait()
     na_all = na[...].reshape(256, D)
     q = nt(na_all, wq[0:QC, :]).astype(BF16)
     k_ = nt(na_all, wq[QC : 2 * QC, :]).astype(BF16)
     v = nt(na_all, wq[2 * QC : 3 * QC, :]).astype(BF16)
+    for right, left in wo_first:
+        right.wait_recv()
+        left.wait_recv()
+    left, right, far = wrap(t - 1, 4), wrap(t + 1, 4), wrap(t + 2, 4)
+    wo_further = [
+        send(wo_part(left, 0, 80), wo_part(left, 0, 80), x_dev(1)),
+        send(wo_part(right, 80, 64), wo_part(right, 80, 64), x_dev(-1)),
+    ]
+    wo_swapped = [send(wo_part(plane, 0, 144), wo_part(plane, 0, 144), core_dev) for plane in (left, right)]
     col = lax.broadcasted_iota(jnp.int32, (1, QC), 1)
     same = (lax.broadcasted_iota(jnp.int32, (256, 256), 0) & 7) == (lax.broadcasted_iota(jnp.int32, (256, 256), 1) & 7)
     total = jnp.zeros((256, QC), F32)
@@ -239,8 +266,36 @@
         weights = jnp.exp(scores - jnp.max(scores, -1, keepdims=True))
         probs = (weights * (1.0 / jnp.sum(weights, -1, keepdims=True))).astype(BF16)
         total = jnp.where(mine, nn(probs, v), total)
-    att[...] = total.astype(BF16)
-    loads[2].wait()
+    att[...] = total.reshape(4, 8, 8, QC).astype(BF16)
+
+    def to_frame(step, j, peer):
+        plane = wrap(t + step, 4)
+        return pltpu.make_async_remote_copy(
+            src_ref=att.at[plane, j], dst_ref=arec.at[t, zh * 2 + core],
+            send_sem=ssem.at[base_m + step * 8 + j], recv_sem=rsem.at[base_m + t * 8 + zh * 2 + core],
+            device_id={"seq": peer, "tensor": plane}, device_id_type=MESH,
+        )
+
+    for step in (2, 1, 3, 0):
+        for a in range(4):
+            for k in range(2):
+                j = a * 2 + k
+                peer = peer_seq(wrap(t + step, 4), a, k)
+                if step:
+                    to_frame(step, j, peer).start()
+                    continue
+
+                @pl.when(peer != s)
+                def _():
+                    to_frame(step, j, peer).start()
+
+                @pl.when(peer == s)
+                def _():
+                    pltpu.make_async_copy(att.at[t, j], arec.at[t, j], rsem.at[base_m + t * 8 + j]).start()
+
+    for copy in wo_further:
+        copy.wait_recv()
+    wo_swapped.append(send(wo_part(far, 0, 144), wo_part(far, 0, 144), core_dev))
 
     def partial_sums(u, product):
         for n in range(3):
@@ -274,31 +329,27 @@
             copy.wait_recv()
         return pf[u, t] + xq[u, 0].astype(F32) + xq[u, 1].astype(F32)
 
-    partial_sums(0, lambda n: nn(att[...], wo[:, n * 384 : n * 384 + 384]))
-    p_first = reduce_first(0)
-
-    p_second = reduce_second(0, p_first)
-
     for copy in turned:
         copy.wait()
     for plane in range(4):
         gflat[plane] = gs[plane].astype(F32).reshape(64, D).astype(BF16)
-    loads[1].wait()
+    loads[2].wait()
     loads[3].wait()
-
-    proj = reduce_third(0, p_second)
-    ms[...] = (hs[t].astype(F32).reshape(64, D) + proj).reshape(8, 8, D).astype(BF16)
-    back = mr.at[zh * 2 + core]
-    exchange(lambda j, peer: ms.at[j], back, base_m)
     g_all = gflat[...].reshape(256, D)
     for n in range(3):
         c = slice(n * 384, n * 384 + 384)
         ga[:, c] = nn(g_all, w2[:, c])
-    for j in range(8):
-        exchange_arrived(back, base_m, j)
-
-    mid_rows = mr[...].astype(F32).reshape(64, D)
-    x_hat2, inv_std2 = normalize(mid_rows)
+    for copy in wo_swapped:
+        copy.wait_recv()
+    for plane in range(4):
+        for j in range(8):
+            slab = arec.at[plane, j]
+            pltpu.make_async_copy(slab, slab, rsem.at[base_m + plane * 8 + j]).wait()
+
+    proj = sum(nn(arec[plane].astype(F32).reshape(64, QC).astype(BF16), wo[plane]) for plane in range(4))
+    mid_rows = (hres[...].astype(F32).reshape(64, D) + proj).astype(BF16)
+    mid[...] = mid_rows
+    x_hat2, inv_std2 = normalize(mid_rows.astype(F32))
     xhat[...] = x_hat2
     inv2[...] = inv_std2
     g2 = gain2[...].reshape(1, D)
@@ -335,11 +386,8 @@
         part = pl.ds(n * 384, 384)
         swapped.append(send(rbuf.at[core, :, part], rbuf.at[2, :, part], core_dev))
 
-    partial_sums(1, lambda n: nt(rbuf[0], w2[n * 384 : n * 384 + 384, :]))
-    d_first = reduce_first(1)
-    partial_sums(2, lambda n: nt(rbuf[1], w1[n * 384 : n * 384 + 384, :]))
-    e_first = reduce_first(2)
-    d_second = reduce_second(1, d_first)
+    partial_sums(0, lambda n: nt(rbuf[0], w2[n * 384 : n * 384 + 384, :]))
+    d_first = reduce_first(0)
     for copy in swapped:
         copy.wait_recv()
 
@@ -360,9 +408,14 @@
     def add(a, b):
         return (a.astype(F32) + b.astype(F32)).astype(BF16)
 
+    HALF = 384
+    halves = (pl.ds(0, HALF), pl.ds(HALF, CB - HALF))
+
     def b_first(u):
         far = wrap(zz + 4, 8)
-        return [send(wb.at[far, u * 2 + d], zb1.at[u, d], z_dev(1 - 2 * d)) for d in range(2)]
+        return [
+            send(wb.at[far, u, :, halves[d]], zb1.at[u, d, :, halves[d]], z_dev(1 - 2 * d)) for d in range(2)
+        ]
 
     def b_step(n, u, copies):
         result = []
@@ -371,21 +424,18 @@
             chunk = wrap(zz + sign * (3 - n), 8)
             copies[d].wait_recv()
             if n == 0:
-                zbs[n, u, d, d] = add(wb[chunk, u * 2 + d], zb1[u, d])
-                zbs[n, u, d, 1 - d] = wb[chunk, u * 2 + 1 - d]
+                taken, other = (slice(0, HALF), slice(HALF, CB))[:: 1 - 2 * d]
+                zbs[n, u, d, :, taken] = add(wb[chunk, u, :, taken], zb1[u, d, :, taken])
+                zbs[n, u, d, :, other] = wb[chunk, u, :, other]
             else:
-                for i in range(2):
-                    zbs[n, u, d, i] = add(wb[chunk, u * 2 + i], zbq[n - 1, u, d, i])
+                zbs[n, u, d] = add(wb[chunk, u], zbq[n - 1, u, d])
             result.append(send(zbs.at[n, u, d], zbq.at[n, u, d], z_dev(sign)))
         return result
 
     def b_last(u, copies):
         for copy in copies:
             copy.wait_recv()
-        for i in range(2):
-            rb[u * 2 + i] = (
-                wb[zz, u * 2 + i].astype(F32) + zbq[2, u, 0, i].astype(F32) + zbq[2, u, 1, i].astype(F32)
-            ).astype(BF16)
+        rb[u] = (wb[zz, u].astype(F32) + zbq[2, u, 0].astype(F32) + zbq[2, u, 1].astype(F32)).astype(BF16)
 
     def a_first():
         far, up, down = wrap(y + 2, 4), wrap(y + 1, 4), wrap(y - 1, 4)
@@ -427,66 +477,27 @@
 
         lax.fori_loop(0, 8, body, 0)
 
-    HALF = 384
-
-    def az_first():
-        far = wrap(zz + 4, 8)
-        up = send(ra.at[far, :, pl.ds(0, HALF)], za1.at[0, :, pl.ds(0, HALF)], z_dev(1))
-        down = send(ra.at[far, :, pl.ds(HALF, CA - HALF)], za1.at[1, :, pl.ds(HALF, CA - HALF)], z_dev(-1))
-        return [up, down]
-
-    def az_step(n, copies):
-        result = []
-        for d in range(2):
-            sign = 1 - 2 * d
-            chunk = wrap(zz + sign * (3 - n), 8)
-            copies[d].wait_recv()
-            if n == 0:
-                taken = slice(0, HALF) if d == 0 else slice(HALF, CA)
-                other = slice(HALF, CA) if d == 0 else slice(0, HALF)
-                zas[n, d, :, taken] = add(ra[chunk, :, taken], za1[d, :, taken])
-                zas[n, d, :, other] = ra[chunk, :, other]
-            else:
-                zas[n, d] = add(ra[chunk], zaq[n - 1, d])
-            result.append(send(zas.at[n, d], zaq.at[n, d], z_dev(sign)))
-        return result
-
-    def az_last(copies):
-        for copy in copies:
+    def straight(rows, place, dev_of, n):
+        return [send(rows.at[place(step)], dev_of[1].at[step - 1], dev_of[0](step)) for step in range(1, n)]
+
+    def straight_sum(rows, here, received, copies):
+        total = rows[here].astype(F32)
+        for i, copy in enumerate(copies):
             copy.wait_recv()
-        return ra[zz].astype(F32) + zaq[2, 0].astype(F32) + zaq[2, 1].astype(F32)
-
-    def by_first():
-        far, up, down = wrap(y + 2, 4), wrap(y + 1, 4), wrap(y - 1, 4)
-        lo, hi = pl.ds(0, 256), pl.ds(256, 256)
-        u1 = send(rb.at[far, :, lo], yb1.at[0], y_dev(1))
-        d1 = send(rb.at[far, :, hi], yb1.at[1], y_dev(-1))
-        u2 = send(rb.at[up, :, hi], ybq.at[0, :, hi], y_dev(1))
-        d2 = send(rb.at[down, :, lo], ybq.at[1, :, lo], y_dev(-1))
-        return u1, d1, u2, d2
-
-    def by_second(copies):
-        up, down = wrap(y + 1, 4), wrap(y - 1, 4)
-        u1, d1, u2, d2 = copies
-        u1.wait_recv()
-        ybs[0] = add(rb[up, :, 0:256], yb1[0])
-        u3 = send(ybs.at[0], ybq.at[0, :, pl.ds(0, 256)], y_dev(1))
-        d1.wait_recv()
-        ybs[1] = add(rb[down, :, 256:512], yb1[1])
-        d3 = send(ybs.at[1], ybq.at[1, :, pl.ds(256, 256)], y_dev(-1))
-        return u2, d2, u3, d3
-
-    def by_last(copies):
-        for copy in copies:
-            copy.wait_recv()
-        return rb[y].astype(F32) + ybq[0].astype(F32) + ybq[1].astype(F32)
+            total = total + received[i].astype(F32)
+        return total
 
     lax.fori_loop(0, 4, grad_b, 0)
-    b1 = [b_first(0), b_first(1)]
+    b1 = [b_first(u) for u in range(4)]
     lax.fori_loop(0, 4, grad_a, 0)
     a1 = a_first()
-    e_second = reduce_second(2, e_first)
-    b2 = [b_step(0, u, b1[u]) for u in range(2)]
+    partial_sums(1, lambda n: nt(rbuf[1], w1[n * 384 : n * 384 + 384, :]))
+    e_first = reduce_first(1)
+    d_second = reduce_second(0, d_first)
+    b2 = [b_step(0, u, b1[u]) for u in range(4)]
+    e_second = reduce_second(1, e_first)
+    b3 = [b_step(1, u, b2[u]) for u in range(4)]
+    a2 = a_second(a1)
 
     def out_view(ref):
         return lambda plane, a: ref.at[pl.ds(peer_seq(plane, a, 0), 2)]
@@ -499,13 +510,12 @@
         return gather_first(out_view(ref), lambda a: None, lambda a: rows.at[pl.ds(a * 2, 2)])
 
     placed = []
-    down_rows = reduce_third(1, d_second)
-    bo[...] = (mr[...].astype(F32).reshape(64, D) + down_rows).reshape(8, 8, D).astype(BF16)
+    down_rows = reduce_third(0, d_second)
+    bo[...] = (mid[...].astype(F32) + down_rows).reshape(8, 8, D).astype(BF16)
     o_first = give(bo, out_b, 0)
-    a2 = a_second(a1)
-    b3 = [b_step(1, u, b2[u]) for u in range(2)]
-
-    scaled = reduce_third(2, e_second) * g2
+    b4 = [b_step(2, u, b3[u]) for u in range(4)]
+
+    scaled = reduce_third(1, e_second) * g2
     x_hat2 = xhat[...]
     plain = jnp.mean(scaled, -1, keepdims=True)
     cross = jnp.mean(scaled * x_hat2, -1, keepdims=True)
@@ -513,20 +523,15 @@
     go[...] = (upstream + inv2[...] * (scaled - plain - x_hat2 * cross)).reshape(8, 8, D).astype(BF16)
     m_first = give(go, out_g, 4)
 
-    b4 = [b_step(2, u, b3[u]) for u in range(2)]
     a_last(a2)
-    az1 = az_first()
-    b_last(0, b4[0])
-    b_last(1, b4[1])
-    by1 = by_first()
+    a3 = straight(ra, lambda step: wrap(zz + step, 8), (z_dev, raq), 8)
     o_further = gather_second(out_view(out_b), o_first)
-    az2 = az_step(0, az1)
-    by2 = by_second(by1)
+    for u in range(4):
+        b_last(u, b4[u])
+    b5 = straight(rb, lambda step: wrap(y + step, 4), (y_dev, rbq), 4)
     m_further = gather_second(out_view(out_g), m_first)
-    az3 = az_step(1, az2)
-    fin_b = by_last(by2)
-    az4 = az_step(2, az3)
-    fin_a = az_last(az4)
+    fin_b = straight_sum(rb, y, rbq, b5)
+    fin_a = straight_sum(ra, zz, raq, a3)
     for c in range(2):
         fin[c, :, 0:CA] = fin_a[c * 18 : c * 18 + 18]
         fin[c, :, CA:] = fin_b[c * 18 : c * 18 + 18]
@@ -559,46 +564,68 @@
         copy.wait()
 
     exchange_sent(lambda j, peer: hid.at[peer], base_h)
-    exchange_sent(lambda j, peer: ms.at[j], base_m)
+    for step in range(4):
+        for a in range(4):
+            for k in range(2):
+                j = a * 2 + k
+                gone = pltpu.make_async_copy(att.at[0, j], att.at[0, j], ssem.at[base_m + step * 8 + j])
+                if step:
+                    gone.wait()
+                    continue
+
+                @pl.when(peer_seq(t, a, k) != s)
+                def _():
+                    gone.wait()
+
     for copy in started:
         copy.wait_send()
 
 
 def place(*refs):
-    sources, results, sems = refs[:4], refs[4:8], refs[8]
+    sources, results, (buf_b, buf_g, buf_1, buf_2, sems) = refs[:4], refs[4:8], refs[8:]
     copies = []
-    for src, dst, parts in zip(sources, results, (4, 4, 1, 1)):
+    for src, dst, buf, parts in zip(sources, results, (buf_b, buf_g, buf_1, buf_2), (4, 4, 1, 1)):
         step = src.shape[0] // parts
         for i in range(parts):
             rows = pl.ds(i * step, step)
-            copies.append(pltpu.make_async_copy(src.at[rows], dst.at[rows], sems.at[len(copies)]))
-    for copy in copies:
-        copy.start()
-    for copy in copies:
-        copy.wait()
+            n = len(copies)
+            copies.append(
+                (
+                    pltpu.make_async_copy(src.at[rows], buf.at[rows], sems.at[0, n]),
+                    pltpu.make_async_copy(buf.at[rows], dst.at[rows], sems.at[1, n]),
+                )
+            )
+    for read, _ in copies:
+        read.start()
+    for read, write in copies:
+        read.wait()
+        write.start()
+    for _, write in copies:
+        write.wait()
 
 
 def local(hidden_in, norm1_gain, qkv_weight, out_weight, norm2_gain, fc1_weight, fc2_weight, out_grad):
     anywhere = pl.BlockSpec(memory_space=pl.ANY)
     vmem = pl.BlockSpec(memory_space=pltpu.VMEM)
     shapes = [
-        ((4, 8, 8, D), BF16), ((4, 8, 8, D), BF16),
-        ((3 * QC, D), BF16), ((QC, D), BF16), ((D, FQ), BF16), ((D, FQ), BF16),
-        ((4, 64, D), BF16), ((256, QC), BF16), ((4, 64, D), BF16), ((256, FQ), F32), ((4, 64, D), BF16),
-        ((3, 4, 64, D), F32), ((3, 4, 64, D), BF16),
-        ((3, 2, 32, D), BF16), ((3, 2, 32, D), BF16), ((3, 2, 64, D), BF16),
-        ((8, 8, D), BF16), ((8, 8, D), BF16), ((64, D), F32), ((64, 1), F32), ((8, 8, D), BF16), ((8, 8, D), BF16),
+        ((4, 8, 8, D), BF16), ((4, 8, 8, D), BF16), ((8, 8, D), BF16),
+        ((3 * QC, D), BF16), ((4, QC, D), BF16), ((D, FQ), BF16), ((D, FQ), BF16),
+        ((4, 64, D), BF16), ((4, 8, 8, QC), BF16), ((4, 8, 8, QC), BF16),
+        ((4, 64, D), BF16), ((256, FQ), F32), ((4, 64, D), BF16),
+        ((2, 4, 64, D), F32), ((2, 4, 64, D), BF16),
+        ((2, 2, 32, D), BF16), ((2, 2, 32, D), BF16), ((2, 2, 64, D), BF16),
+        ((64, D), BF16), ((64, D), F32), ((64, 1), F32), ((8, 8, D), BF16), ((8, 8, D), BF16),
         ((ROWS, D), BF16), ((3, ROWS, 256), BF16), ((3, 256, FQ), BF16),
         ((4, 8, SLAB, CA), BF16), ((2, 4, SLAB, CA), BF16), ((2, 4, SLAB, CA), BF16), ((2, 8, SLAB, CA), BF16),
-        ((8, SLAB, CA), BF16), ((2, SLAB, CA), BF16), ((3, 2, SLAB, CA), BF16), ((3, 2, SLAB, CA), BF16),
-        ((8, 4, SLAB, CB), BF16), ((2, 2, SLAB, CB), BF16), ((3, 2, 2, 2, SLAB, CB), BF16), ((3, 2, 2, 2, SLAB, CB), BF16),
-        ((4, SLAB, CB), BF16), ((2, SLAB, 256), BF16), ((2, SLAB, 256), BF16), ((2, SLAB, CB), BF16),
+        ((8, SLAB, CA), BF16), ((7, SLAB, CA), BF16),
+        ((8, 4, SLAB, CB), BF16), ((4, 2, SLAB, CB), BF16), ((3, 4, 2, SLAB, CB), BF16), ((3, 4, 2, SLAB, CB), BF16),
+        ((4, SLAB, CB), BF16), ((3, SLAB, CB), BF16),
         ((2, 18, FQ), F32),
     ]
     scratch = [pltpu.VMEM(shape, kind) for shape, kind in shapes]
     scratch += [
         pltpu.SemaphoreType.DMA((N_SEM,)), pltpu.SemaphoreType.DMA((N_SEM,)),
-        pltpu.SemaphoreType.DMA((4,)), pltpu.SemaphoreType.DMA((16,)), pltpu.SemaphoreType.DMA((8,)),
+        pltpu.SemaphoreType.DMA((4,)), pltpu.SemaphoreType.DMA((20,)), pltpu.SemaphoreType.DMA((8,)),
         pltpu.SemaphoreType.DMA,
     ]
     results = [
@@ -631,7 +658,8 @@
         out_shape=results,
         in_specs=[anywhere] * 4,
         out_specs=[anywhere] * 4,
-        scratch_shapes=[pltpu.SemaphoreType.DMA((10,))],
+        scratch_shapes=[pltpu.VMEM(made_one.shape, made_one.dtype) for made_one in results]
+        + [pltpu.SemaphoreType.DMA((2, 10))],
         compiler_params=pltpu.CompilerParams(vmem_limit_bytes=60 * 1024 * 1024),
     )(*made)
     shape = hidden_in.shape

time: 143 us -> 95 us (0.66)
  Pallas kernels: 142 us -> 94.1 us
    pallas_call x1, Pallas kernels: 43.6 us -> 2.25 us  [local(): pl.pallas_call(place, out_shape=results, in_specs=[anywhere] * 4, out_spe...]
    pallas_call x1, Pallas kernels: 98.7 us -> 91.8 us  [local(): pl.pallas_call(kernel, out_shape=results, in_specs=[anywhere, vmem, anywh...]
where the time goes in v3:
time: 95 us; the launch traced here: 94.9 us
  Pallas kernels  94.1 us (99%)
    pallas_call x1, Pallas kernels, local(): pl.pallas_call(kernel, out_shape=results, in_specs=[anywhere, vmem, anywh...  91.8 us
    pallas_call x1, Pallas kernels, local(): pl.pallas_call(place, out_shape=results, in_specs=[anywhere] * 4, out_spe...  2.25 us

profile of v3, /device:TPU:1, one launch (start us, length us, event | category | flops | bytes accessed | tf_op | source)
XLA Modules:
  0.0 94.9 jit_solution(10661975630166702579)
XLA Ops:
  0.6 91.8 %shard_map.111 = (bf16[32,8,1152]{2,1,0:T(8,128)(2,1)}, bf16[32,8,1152]{2,1,0:T(8,128)(2,1)}, f32[18,1152]{1,0:T(8,128)}, f32[18,1152]{1,0:T(8,128)}) custom-call(bf16[32,8,1152]{2,1,0:T(8,128)(2,1)} %bitcast.8, f32[1152]{0:T(1024)} %gain1.1, bf16[864,1152]{1,0:T(8,128)(2,1)} %bitcast.7, bf16[288,1152]{1,0:T(8,128)(2,1)} %wo_h.1, f32[1152]{0:T(1024)} %gain2.1, ...), custom_call_target="tpu_custom_call" | custom-call | tf_op jit(solution)/shard_map/pallas_call | solution.py:637
  92.5 2.3 %shard_map.112 = (bf16[32,8,1152]{2,1,0:T(8,128)(2,1)}, bf16[32,8,1152]{2,1,0:T(8,128)(2,1)}, f32[18,1152]{1,0:T(8,128)}, f32[18,1152]{1,0:T(8,128)}) custom-call(bf16[32,8,1152]{2,1,0:T(8,128)(2,1)} %get-tuple-element.12.refs_0_, bf16[32,8,1152]{2,1,0:T(8,128)(2,1)} %get-tuple-element.13.refs_1_, f32[18,1152]{1,0:T(8,128)} %get-tuple-element.14.refs_2_, ...), custom_call_target="tpu_custom_call" | custom-call | tf_op jit(solution)/shard_map/pallas_call | solution.py:656

commit v4 on v3

--- a/solution.py
+++ b/solution.py
@@ -21,7 +21,7 @@
 CA = 512
 CB = 640
 EPS = 1e-06
-N_SEM = 200
+N_SEM = 224
 
 
 def slab_sources(first, count):
@@ -51,7 +51,7 @@
 def kernel(
     hid, gain1, wq_h, wo_h, gain2, w1_h, w2_h, og,
     out_b, out_g, out_1, out_2,
-    hs, gs, hres, wq, wo, w1, w2, na, att, arec, gflat, ga, nb,
+    hl, gs, hres, wq, wo, w1, w2, na, qkv, qrec, att, arec, gflat, ga, nb,
     pf, pb, xr1, xs2, xq, mid, xhat, inv2, bo, go,
     perm, lbuf, rbuf,
     wa, ya1, yas, yaq, ra, raq,
@@ -85,25 +85,35 @@
         return a * 8 + wrap(plane - zh - y - a, 4) * 2 + k
 
     barrier = pltpu.get_barrier_semaphore()
-    for dev in (x_dev(1), x_dev(-1), core_dev):
+    for dev in (x_dev(1), x_dev(-1), z_dev(1), z_dev(-1), z_dev(3), z_dev(-3)):
         pl.semaphore_signal(barrier, inc=1, device_id=dev, device_id_type=MESH)
+    for other in range(32):
+        pl.semaphore_signal(barrier, inc=1, device_id={"seq": other}, device_id_type=MESH)
     for step in range(1, 4):
-        pl.semaphore_signal(barrier, inc=1, device_id=y_dev(step), device_id_type=MESH)
-    for step in range(1, 8):
-        pl.semaphore_signal(barrier, inc=1, device_id=z_dev(step), device_id_type=MESH)
-    for plane in range(4):
         for a in range(4):
             for k in range(2):
-                dev = {"seq": peer_seq(t, a, k), "tensor": plane}
+                dev = {"seq": peer_seq(t, a, k), "tensor": wrap(t + step, 4)}
                 pl.semaphore_signal(barrier, inc=1, device_id=dev, device_id_type=MESH)
 
     loads = [
         pltpu.make_async_copy(src, dst, lsem.at[i])
-        for i, (src, dst) in enumerate(((wo_h, wo.at[t]), (wq_h, wq), (w2_h, w2), (w1_h, w1)))
+        for i, (src, dst) in enumerate(((hid, hl), (wq_h, wq), (wo_h, wo.at[t]), (w2_h, w2), (w1_h, w1)))
     ]
     for load in loads:
         load.start()
-    pl.semaphore_wait(barrier, 45)
+
+    g1 = gain1[...].reshape(1, D)
+    loads[0].wait()
+
+    def norm_rows(i, carry):
+        x_hat, _ = normalize(hl[pl.ds(i * 8, 8)].astype(F32).reshape(64, D))
+        na[i] = (x_hat * g1).astype(BF16)
+        return carry
+
+    lax.fori_loop(0, 4, norm_rows, 0)
+    loads[1].wait()
+    qkv[...] = nt(na[...].reshape(256, D), wq[...]).reshape(32, 8, 3 * QC).astype(BF16)
+    pl.semaphore_wait(barrier, 62)
 
     count = [0]
     started = []
@@ -122,41 +132,23 @@
         started.append(copy)
         return copy
 
-    def exchange(src_of, dst, base):
-        for a in range(4):
-            for k in range(2):
-                j = a * 2 + k
-                peer = peer_seq(t, a, k)
-                src = src_of(j, peer)
-
-                @pl.when(peer != s)
-                def _():
-                    pltpu.make_async_remote_copy(
-                        src_ref=src, dst_ref=dst, send_sem=ssem.at[base + j], recv_sem=rsem.at[base + zh * 2 + core],
-                        device_id={"seq": peer}, device_id_type=MESH,
-                    ).start()
-
-                @pl.when(peer == s)
-                def _():
-                    pltpu.make_async_copy(src, dst, rsem.at[base + j]).start()
-
-    def exchange_arrived(dst, base, j):
-        pltpu.make_async_copy(dst, dst, rsem.at[base + j]).wait()
-
-    def exchange_sent(src_of, base):
-        for a in range(4):
-            for k in range(2):
-                j = a * 2 + k
-                peer = peer_seq(t, a, k)
-                src = src_of(j, peer)
-
-                @pl.when(peer != s)
-                def _():
-                    pltpu.make_async_copy(src, src, ssem.at[base + j]).wait()
-
-    base_h, base_m = fresh(8), fresh(32)
-    here = hs.at[t, zh * 2 + core]
-    exchange(lambda j, peer: hid.at[peer], here, base_h)
+    base_h, base_m = fresh(32), fresh(32)
+
+    def to_patches(other):
+        return pltpu.make_async_remote_copy(
+            src_ref=qkv.at[other], dst_ref=qrec.at[s], send_sem=ssem.at[base_h + other], recv_sem=rsem.at[base_h + s],
+            device_id={"seq": other}, device_id_type=MESH,
+        )
+
+    for other in range(32):
+
+        @pl.when(s != other)
+        def _():
+            to_patches(other).start()
+
+        @pl.when(s == other)
+        def _():
+            pltpu.make_async_copy(qkv.at[other], qrec.at[other], rsem.at[base_h + other]).start()
 
     turned = [
         pltpu.make_async_copy(
@@ -171,13 +163,8 @@
     for copy in turned:
         copy.start()
 
-    def gather_first(view, arrived, own=None):
-        copies = []
-        for a in range(4):
-            arrived(a)
-            src = view(t, a) if own is None else own(a)
-            copies.append((send(src, view(t, a), x_dev(1)), send(src, view(t, a), x_dev(-1))))
-        return copies
+    def gather_first(view, own):
+        return [(send(own(a), view(t, a), x_dev(1)), send(own(a), view(t, a), x_dev(-1))) for a in range(4)]
 
     def gather_second(view, copies):
         left, right = wrap(t - 1, 4), wrap(t + 1, 4)
@@ -196,16 +183,6 @@
         for copy in further:
             copy.wait_recv()
 
-    def pair(ref):
-        return lambda plane, a: ref.at[plane, pl.ds(a * 2, 2)]
-
-    def slabs_arrived(dst, base):
-        def arrived(a):
-            for k in range(2):
-                exchange_arrived(dst, base, a * 2 + k)
-
-        return arrived
-
     def wo_part(plane, first, size):
         return wo.at[plane, pl.ds(pl.multiple_of(core * 144 + first, 16), size)]
 
@@ -213,8 +190,8 @@
         src = wo_part(t, first, size)
         return send(src, src, x_dev(1)), send(src, src, x_dev(-1))
 
-    loads[0].wait()
-    wo_first = [wo_send(0, 48)]
+    loads[2].wait()
+    wo_first = wo_send(0, 144)
 
     def make_perm(i, carry):
         first = pl.multiple_of(i * 128, 128)
@@ -226,35 +203,21 @@
 
     lax.fori_loop(0, ROWS // 128, make_perm, 0)
 
-    g1 = gain1[...].reshape(1, D)
-
-    def norm_share(plane):
-        x_hat, _ = normalize(hs[plane].astype(F32).reshape(64, D))
-        na[plane] = (x_hat * g1).astype(BF16)
-
-    h_first = gather_first(pair(hs), slabs_arrived(here, base_h))
-    norm_share(t)
-    h_further = gather_second(pair(hs), h_first)
-    wo_first.append(wo_send(48, 96))
-    norm_share(wrap(t - 1, 4))
-    norm_share(wrap(t + 1, 4))
-    gather_third(h_further)
-    norm_share(wrap(t + 2, 4))
-
-    loads[1].wait()
-    na_all = na[...].reshape(256, D)
-    q = nt(na_all, wq[0:QC, :]).astype(BF16)
-    k_ = nt(na_all, wq[QC : 2 * QC, :]).astype(BF16)
-    v = nt(na_all, wq[2 * QC : 3 * QC, :]).astype(BF16)
-    for right, left in wo_first:
-        right.wait_recv()
-        left.wait_recv()
+    wo_first[0].wait_recv()
+    wo_first[1].wait_recv()
     left, right, far = wrap(t - 1, 4), wrap(t + 1, 4), wrap(t + 2, 4)
     wo_further = [
         send(wo_part(left, 0, 80), wo_part(left, 0, 80), x_dev(1)),
         send(wo_part(right, 80, 64), wo_part(right, 80, 64), x_dev(-1)),
     ]
     wo_swapped = [send(wo_part(plane, 0, 144), wo_part(plane, 0, 144), core_dev) for plane in (left, right)]
+
+    for other in range(32):
+        slab = qrec.at[other]
+        pltpu.make_async_copy(slab, slab, rsem.at[base_h + other]).wait()
+    q = qrec[:, :, 0:QC].reshape(256, QC)
+    k_ = qrec[:, :, QC : 2 * QC].reshape(256, QC)
+    v = qrec[:, :, 2 * QC : 3 * QC].reshape(256, QC)
     col = lax.broadcasted_iota(jnp.int32, (1, QC), 1)
     same = (lax.broadcasted_iota(jnp.int32, (256, 256), 0) & 7) == (lax.broadcasted_iota(jnp.int32, (256, 256), 1) & 7)
     total = jnp.zeros((256, QC), F32)
@@ -266,32 +229,29 @@
         weights = jnp.exp(scores - jnp.max(scores, -1, keepdims=True))
         probs = (weights * (1.0 / jnp.sum(weights, -1, keepdims=True))).astype(BF16)
         total = jnp.where(mine, nn(probs, v), total)
-    att[...] = total.reshape(4, 8, 8, QC).astype(BF16)
-
-    def to_frame(step, j, peer):
-        plane = wrap(t + step, 4)
+    att[...] = total.reshape(32, 8, QC).astype(BF16)
+
+    def plane_of(frame):
+        return lax.rem(frame // 8 + frame // 2 % 4 + zh + y, 4)
+
+    def to_frame(frame):
         return pltpu.make_async_remote_copy(
-            src_ref=att.at[plane, j], dst_ref=arec.at[t, zh * 2 + core],
-            send_sem=ssem.at[base_m + step * 8 + j], recv_sem=rsem.at[base_m + t * 8 + zh * 2 + core],
-            device_id={"seq": peer, "tensor": plane}, device_id_type=MESH,
+            src_ref=att.at[frame], dst_ref=arec.at[t, zh * 2 + core],
+            send_sem=ssem.at[base_m + frame], recv_sem=rsem.at[base_m + t * 8 + zh * 2 + core],
+            device_id={"seq": frame, "tensor": plane_of(frame)}, device_id_type=MESH,
         )
 
-    for step in (2, 1, 3, 0):
-        for a in range(4):
-            for k in range(2):
-                j = a * 2 + k
-                peer = peer_seq(wrap(t + step, 4), a, k)
-                if step:
-                    to_frame(step, j, peer).start()
-                    continue
-
-                @pl.when(peer != s)
-                def _():
-                    to_frame(step, j, peer).start()
-
-                @pl.when(peer == s)
-                def _():
-                    pltpu.make_async_copy(att.at[t, j], arec.at[t, j], rsem.at[base_m + t * 8 + j]).start()
+    for frame in range(32):
+        stays = jnp.logical_and(s == frame, plane_of(frame) == t)
+
+        @pl.when(jnp.logical_not(stays))
+        def _():
+            to_frame(frame).start()
+
+        @pl.when(stays)
+        def _():
+            here = arec.at[t, zh * 2 + core]
+            pltpu.make_async_copy(att.at[frame], here, rsem.at[base_m + t * 8 + zh * 2 + core]).start()
 
     for copy in wo_further:
         copy.wait_recv()
@@ -333,8 +293,8 @@
         copy.wait()
     for plane in range(4):
         gflat[plane] = gs[plane].astype(F32).reshape(64, D).astype(BF16)
-    loads[2].wait()
     loads[3].wait()
+    loads[4].wait()
     g_all = gflat[...].reshape(256, D)
     for n in range(3):
         c = slice(n * 384, n * 384 + 384)
@@ -358,7 +318,7 @@
     def quarter(ref):
         return lambda plane, a: ref.at[plane, pl.ds(a * 16, 16)]
 
-    n_first = gather_first(quarter(nb), lambda a: None)
+    n_first = gather_first(quarter(nb), lambda a: quarter(nb)(t, a))
 
     for n in range(2):
         c = slice(n * 640, n * 640 + 640)
@@ -507,7 +467,7 @@
             copy = pltpu.make_async_copy(rows.at[pl.ds(a * 2, 2)], out_view(ref)(t, a), osem.at[base + a])
             copy.start()
             placed.append(copy)
-        return gather_first(out_view(ref), lambda a: None, lambda a: rows.at[pl.ds(a * 2, 2)])
+        return gather_first(out_view(ref), lambda a: rows.at[pl.ds(a * 2, 2)])
 
     placed = []
     down_rows = reduce_third(0, d_second)
@@ -563,19 +523,15 @@
     for copy in placed:
         copy.wait()
 
-    exchange_sent(lambda j, peer: hid.at[peer], base_h)
-    for step in range(4):
-        for a in range(4):
-            for k in range(2):
-                j = a * 2 + k
-                gone = pltpu.make_async_copy(att.at[0, j], att.at[0, j], ssem.at[base_m + step * 8 + j])
-                if step:
-                    gone.wait()
-                    continue
-
-                @pl.when(peer_seq(t, a, k) != s)
-                def _():
-                    gone.wait()
+    for other in range(32):
+
+        @pl.when(s != other)
+        def _():
+            to_patches(other).wait_send()
+
+        @pl.when(jnp.logical_not(jnp.logical_and(s == other, plane_of(other) == t)))
+        def _():
+            to_frame(other).wait_send()
 
     for copy in started:
         copy.wait_send()
@@ -608,9 +564,10 @@
     anywhere = pl.BlockSpec(memory_space=pl.ANY)
     vmem = pl.BlockSpec(memory_space=pltpu.VMEM)
     shapes = [
-        ((4, 8, 8, D), BF16), ((4, 8, 8, D), BF16), ((8, 8, D), BF16),
+        ((32, 8, D), BF16), ((4, 8, 8, D), BF16), ((8, 8, D), BF16),
         ((3 * QC, D), BF16), ((4, QC, D), BF16), ((D, FQ), BF16), ((D, FQ), BF16),
-        ((4, 64, D), BF16), ((4, 8, 8, QC), BF16), ((4, 8, 8, QC), BF16),
+        ((4, 64, D), BF16), ((32, 8, 3 * QC), BF16), ((32, 8, 3 * QC), BF16),
+        ((32, 8, QC), BF16), ((4, 8, 8, QC), BF16),
         ((4, 64, D), BF16), ((256, FQ), F32), ((4, 64, D), BF16),
         ((2, 4, 64, D), F32), ((2, 4, 64, D), BF16),
         ((2, 2, 32, D), BF16), ((2, 2, 32, D), BF16), ((2, 2, 64, D), BF16),
@@ -625,7 +582,7 @@
     scratch = [pltpu.VMEM(shape, kind) for shape, kind in shapes]
     scratch += [
         pltpu.SemaphoreType.DMA((N_SEM,)), pltpu.SemaphoreType.DMA((N_SEM,)),
-        pltpu.SemaphoreType.DMA((4,)), pltpu.SemaphoreType.DMA((20,)), pltpu.SemaphoreType.DMA((8,)),
+        pltpu.SemaphoreType.DMA((5,)), pltpu.SemaphoreType.DMA((20,)), pltpu.SemaphoreType.DMA((8,)),
         pltpu.SemaphoreType.DMA,
     ]
     results = [

time: 95 us -> 89.6 us (0.943); the launches traced: 94.9 us -> 88.2 us
  Pallas kernels: 94.1 us -> 87.4 us
    pallas_call x1, Pallas kernels: 91.8 us -> 85.2 us  [local(): pl.pallas_call(kernel, out_shape=results, in_specs=[anywhere, vmem, anywh...]
where the time goes in v4:
time: 89.6 us; the launch traced here: 88.2 us
  Pallas kernels  87.4 us (98%)
    pallas_call x1, Pallas kernels, local(): pl.pallas_call(kernel, out_shape=results, in_specs=[anywhere, vmem, anywh...  85.2 us
    pallas_call x1, Pallas kernels, local(): pl.pallas_call(place, out_shape=results, in_specs=[anywhere] * 4, out_spe...  2.25 us

profile of v4, /device:TPU:1, one launch (start us, length us, event | category | flops | bytes accessed | tf_op | source)
XLA Modules:
  0.0 88.2 jit_solution(2675571983583185433)
XLA Ops:
  0.6 85.2 %shard_map.111 = (bf16[32,8,1152]{2,1,0:T(8,128)(2,1)}, bf16[32,8,1152]{2,1,0:T(8,128)(2,1)}, f32[18,1152]{1,0:T(8,128)}, f32[18,1152]{1,0:T(8,128)}) custom-call(bf16[32,8,1152]{2,1,0:T(8,128)(2,1)} %bitcast.8, f32[1152]{0:T(1024)} %gain1.1, bf16[864,1152]{1,0:T(8,128)(2,1)} %bitcast.7, bf16[288,1152]{1,0:T(8,128)(2,1)} %wo_h.1, f32[1152]{0:T(1024)} %gain2.1, ...), custom_call_target="tpu_custom_call" | custom-call | tf_op jit(solution)/shard_map/pallas_call | solution.py:594
  85.8 2.3 %shard_map.112 = (bf16[32,8,1152]{2,1,0:T(8,128)(2,1)}, bf16[32,8,1152]{2,1,0:T(8,128)(2,1)}, f32[18,1152]{1,0:T(8,128)}, f32[18,1152]{1,0:T(8,128)}) custom-call(bf16[32,8,1152]{2,1,0:T(8,128)(2,1)} %get-tuple-element.12.refs_0_, bf16[32,8,1152]{2,1,0:T(8,128)(2,1)} %get-tuple-element.13.refs_1_, f32[18,1152]{1,0:T(8,128)} %get-tuple-element.14.refs_2_, ...), custom_call_target="tpu_custom_call" | custom-call | tf_op jit(solution)/shard_map/pallas_call | solution.py:613

commit v5 on v4

--- a/solution.py
+++ b/solution.py
@@ -16,22 +16,23 @@
 D = 1152
 FQ = 1152
 QC = 288
-SLAB = 40
+SLAB = 36
 ROWS = 32 * SLAB
 CA = 512
 CB = 640
+CA2 = CA // 2
+NB = CB // 128
 EPS = 1e-06
 N_SEM = 224
 
 
 def slab_sources(first, count):
     n = lax.broadcasted_iota(jnp.int32, (count, 1), 0) + first
-    slab = (n * 1639) >> 16
+    slab = (n * 1821) >> 16
     within = n - slab * SLAB
     core = jnp.where(within >= 18, 1, 0)
     z, y = slab >> 2, slab & 3
-    source = (((z >> 1) * 4 + y) * 2 + core) * 36 + (z & 1) * 18 + within - core * 18
-    return jnp.where(within < 36, source, -1)
+    return (((z >> 1) * 4 + y) * 2 + core) * 36 + (z & 1) * 18 + within - core * 18
 
 
 def nn(a, b):
@@ -99,7 +100,7 @@
         pltpu.make_async_copy(src, dst, lsem.at[i])
         for i, (src, dst) in enumerate(((hid, hl), (wq_h, wq), (wo_h, wo.at[t]), (w2_h, w2), (w1_h, w1)))
     ]
-    for load in loads:
+    for load in loads[:2]:
         load.start()
 
     g1 = gain1[...].reshape(1, D)
@@ -112,6 +113,8 @@
 
     lax.fori_loop(0, 4, norm_rows, 0)
     loads[1].wait()
+    for load in loads[2:]:
+        load.start()
     qkv[...] = nt(na[...].reshape(256, D), wq[...]).reshape(32, 8, 3 * QC).astype(BF16)
     pl.semaphore_wait(barrier, 62)
 
@@ -164,7 +167,11 @@
         copy.start()
 
     def gather_first(view, own):
-        return [(send(own(a), view(t, a), x_dev(1)), send(own(a), view(t, a), x_dev(-1))) for a in range(4)]
+        ups, downs = [None] * 4, [None] * 4
+        for up, down in ((0, 2), (1, 3), (2, 0), (3, 1)):
+            ups[up] = send(own(up), view(t, up), x_dev(1))
+            downs[down] = send(own(down), view(t, down), x_dev(-1))
+        return list(zip(ups, downs))
 
     def gather_second(view, copies):
         left, right = wrap(t - 1, 4), wrap(t + 1, 4)
@@ -320,14 +327,14 @@
 
     n_first = gather_first(quarter(nb), lambda a: quarter(nb)(t, a))
 
-    for n in range(2):
-        c = slice(n * 640, n * 640 + 640)
+    for n in range(3):
+        c = slice(n * 384, n * 384 + 384)
         lbuf[0, c, :] = nt(perm[c, :], g_all).astype(BF16)
     n_further = gather_second(quarter(nb), n_first)
     gather_third(n_further)
     nb_all = nb[...].reshape(256, D)
-    for n in range(2):
-        c = slice(n * 640, n * 640 + 640)
+    for n in range(3):
+        c = slice(n * 384, n * 384 + 384)
         lbuf[1, c, :] = nt(perm[c, :], nb_all).astype(BF16)
 
     swapped = [send(lbuf.at[core], lbuf.at[2], core_dev)]
@@ -352,29 +359,31 @@
         copy.wait_recv()
 
     def grad_b(i, carry):
-        rows = pl.ds(pl.multiple_of(i * 320, 320), 320)
+        rows = pl.ds(pl.multiple_of(i * 288, 32), 288)
         value = nn(lbuf[kept, rows, :], rbuf[kept, :, CA:]) + nn(lbuf[2, rows, :], rbuf[2, :, CA:])
-        for m in range(8):
-            wb[i * 2 + m // 4, m % 4] = value[m * SLAB : (m + 1) * SLAB].astype(BF16)
+        for m in range(2):
+            for u in range(NB):
+                wb[u, i * 2 + m] = value[m * 144 : (m + 1) * 144, u * 128 : (u + 1) * 128].astype(BF16)
         return carry
 
     def grad_a(i, carry):
-        rows = pl.ds(pl.multiple_of(i * 320, 320), 320)
+        rows = pl.ds(pl.multiple_of(i * 288, 32), 288)
         value = nn(lbuf[kept, rows, :], rbuf[kept, :, :CA]) + nn(lbuf[2, rows, :], rbuf[2, :, :CA])
         for m in range(8):
-            wa[m % 4, i * 2 + m // 4] = value[m * SLAB : (m + 1) * SLAB].astype(BF16)
+            for u in range(2):
+                part = value[m * SLAB : (m + 1) * SLAB, u * CA2 : (u + 1) * CA2]
+                wa[u, m % 4, i * 2 + m // 4] = part.astype(BF16)
         return carry
 
     def add(a, b):
         return (a.astype(F32) + b.astype(F32)).astype(BF16)
 
-    HALF = 384
-    halves = (pl.ds(0, HALF), pl.ds(HALF, CB - HALF))
+    halves = (pl.ds(0, 80), pl.ds(80, 64))
 
     def b_first(u):
         far = wrap(zz + 4, 8)
         return [
-            send(wb.at[far, u, :, halves[d]], zb1.at[u, d, :, halves[d]], z_dev(1 - 2 * d)) for d in range(2)
+            send(wb.at[u, far, halves[d]], zb1.at[u, d, halves[d]], z_dev(1 - 2 * d)) for d in range(2)
         ]
 
     def b_step(n, u, copies):
@@ -384,80 +393,87 @@
             chunk = wrap(zz + sign * (3 - n), 8)
             copies[d].wait_recv()
             if n == 0:
-                taken, other = (slice(0, HALF), slice(HALF, CB))[:: 1 - 2 * d]
-                zbs[n, u, d, :, taken] = add(wb[chunk, u, :, taken], zb1[u, d, :, taken])
-                zbs[n, u, d, :, other] = wb[chunk, u, :, other]
+                taken, other = (slice(0, 80), slice(80, 144))[:: 1 - 2 * d]
+                zbs[n, u, d, taken, :] = add(wb[u, chunk, taken, :], zb1[u, d, taken, :])
+                zbs[n, u, d, other, :] = wb[u, chunk, other, :]
             else:
-                zbs[n, u, d] = add(wb[chunk, u], zbq[n - 1, u, d])
+                zbs[n, u, d] = add(wb[u, chunk], zbq[n - 1, u, d])
             result.append(send(zbs.at[n, u, d], zbq.at[n, u, d], z_dev(sign)))
         return result
 
     def b_last(u, copies):
         for copy in copies:
             copy.wait_recv()
-        rb[u] = (wb[zz, u].astype(F32) + zbq[2, u, 0].astype(F32) + zbq[2, u, 1].astype(F32)).astype(BF16)
-
-    def a_first():
+        total = wb[u, zz].astype(F32) + zbq[2, u, 0].astype(F32) + zbq[2, u, 1].astype(F32)
+        for i in range(4):
+            rb[u, i] = total[i * SLAB : (i + 1) * SLAB].astype(BF16)
+
+    def a_first(u):
         far, up, down = wrap(y + 2, 4), wrap(y + 1, 4), wrap(y - 1, 4)
         lo, hi = pl.ds(0, 4), pl.ds(4, 4)
-        u1 = send(wa.at[far, lo], ya1.at[0], y_dev(1))
-        d1 = send(wa.at[far, hi], ya1.at[1], y_dev(-1))
-        u2 = send(wa.at[up, hi], yaq.at[0, hi], y_dev(1))
-        d2 = send(wa.at[down, lo], yaq.at[1, lo], y_dev(-1))
+        u1 = send(wa.at[u, far, lo], ya1.at[u, 0], y_dev(1))
+        d1 = send(wa.at[u, far, hi], ya1.at[u, 1], y_dev(-1))
+        u2 = send(wa.at[u, up, hi], yaq.at[u, 0, hi], y_dev(1))
+        d2 = send(wa.at[u, down, lo], yaq.at[u, 1, lo], y_dev(-1))
         return u1, d1, u2, d2
 
-    def a_second(copies):
+    def a_second(u, copies):
         up, down = wrap(y + 1, 4), wrap(y - 1, 4)
         u1, d1, u2, d2 = copies
         u1.wait_recv()
 
         def body_up(i, carry):
-            yas[0, i] = add(wa[up, i], ya1[0, i])
+            yas[u, 0, i] = add(wa[u, up, i], ya1[u, 0, i])
             return carry
 
         lax.fori_loop(0, 4, body_up, 0)
-        u3 = send(yas.at[0], yaq.at[0, pl.ds(0, 4)], y_dev(1))
+        u3 = send(yas.at[u, 0], yaq.at[u, 0, pl.ds(0, 4)], y_dev(1))
         d1.wait_recv()
 
         def body_down(i, carry):
-            yas[1, i] = add(wa[down, i + 4], ya1[1, i])
+            yas[u, 1, i] = add(wa[u, down, i + 4], ya1[u, 1, i])
             return carry
 
         lax.fori_loop(0, 4, body_down, 0)
-        d3 = send(yas.at[1], yaq.at[1, pl.ds(4, 4)], y_dev(-1))
+        d3 = send(yas.at[u, 1], yaq.at[u, 1, pl.ds(4, 4)], y_dev(-1))
         return u2, d2, u3, d3
 
-    def a_last(copies):
+    def a_last(u, copies):
         for copy in copies:
             copy.wait_recv()
 
         def body(i, carry):
-            ra[i] = (wa[y, i].astype(F32) + yaq[0, i].astype(F32) + yaq[1, i].astype(F32)).astype(BF16)
+            total = wa[u, y, i].astype(F32) + yaq[u, 0, i].astype(F32) + yaq[u, 1, i].astype(F32)
+            ra[u, i] = total.astype(BF16)
             return carry
 
         lax.fori_loop(0, 8, body, 0)
 
-    def straight(rows, place, dev_of, n):
-        return [send(rows.at[place(step)], dev_of[1].at[step - 1], dev_of[0](step)) for step in range(1, n)]
-
-    def straight_sum(rows, here, received, copies):
+    def straight(rows, received, dev_of, here, n):
+        return [
+            send(rows.at[wrap(here + step, n)], received.at[step - 1], dev_of(step)) for step in (n // 2, *range(1, n // 2), *range(n // 2 + 1, n))
+        ]
+
+    def straight_sum(rows, received, here, copies):
+        for copy in copies:
+            copy.wait_recv()
         total = rows[here].astype(F32)
-        for i, copy in enumerate(copies):
-            copy.wait_recv()
+        for i in range(len(copies)):
             total = total + received[i].astype(F32)
         return total
 
+    lax.fori_loop(0, 4, grad_a, 0)
+    a1 = [a_first(u) for u in range(2)]
     lax.fori_loop(0, 4, grad_b, 0)
-    b1 = [b_first(u) for u in range(4)]
-    lax.fori_loop(0, 4, grad_a, 0)
-    a1 = a_first()
+    b1 = [b_first(u) for u in range(NB)]
     partial_sums(1, lambda n: nt(rbuf[1], w1[n * 384 : n * 384 + 384, :]))
     e_first = reduce_first(1)
     d_second = reduce_second(0, d_first)
-    b2 = [b_step(0, u, b1[u]) for u in range(4)]
+    b2 = [b_step(0, u, b1[u]) for u in range(NB)]
+    a2 = [a_second(0, a1[0])]
     e_second = reduce_second(1, e_first)
-    b3 = [b_step(1, u, b2[u]) for u in range(4)]
-    a2 = a_second(a1)
+    a2.append(a_second(1, a1[1]))
+    b3 = [b_step(1, u, b2[u]) for u in range(NB)]
 
     def out_view(ref):
         return lambda plane, a: ref.at[pl.ds(peer_seq(plane, a, 0), 2)]
@@ -473,7 +489,7 @@
     down_rows = reduce_third(0, d_second)
     bo[...] = (mid[...].astype(F32) + down_rows).reshape(8, 8, D).astype(BF16)
     o_first = give(bo, out_b, 0)
-    b4 = [b_step(2, u, b3[u]) for u in range(4)]
+    b4 = [b_step(2, u, b3[u]) for u in range(NB)]
 
     scaled = reduce_third(1, e_second) * g2
     x_hat2 = xhat[...]
@@ -483,18 +499,23 @@
     go[...] = (upstream + inv2[...] * (scaled - plain - x_hat2 * cross)).reshape(8, 8, D).astype(BF16)
     m_first = give(go, out_g, 4)
 
-    a_last(a2)
-    a3 = straight(ra, lambda step: wrap(zz + step, 8), (z_dev, raq), 8)
+    a3 = []
+    for u in range(2):
+        a_last(u, a2[u])
+        a3.append(straight(ra.at[u], raq.at[u], z_dev, zz, 8))
     o_further = gather_second(out_view(out_b), o_first)
-    for u in range(4):
+    b5 = []
+    for u in range(NB):
         b_last(u, b4[u])
-    b5 = straight(rb, lambda step: wrap(y + step, 4), (y_dev, rbq), 4)
+        b5.append(straight(rb.at[u], rbq.at[u], y_dev, y, 4))
     m_further = gather_second(out_view(out_g), m_first)
-    fin_b = straight_sum(rb, y, rbq, b5)
-    fin_a = straight_sum(ra, zz, raq, a3)
+    sums = [
+        *(((u * CA2, CA2), straight_sum(ra.at[u], raq.at[u], zz, a3[u])) for u in range(2)),
+        *(((CA + u * 128, 128), straight_sum(rb.at[u], rbq.at[u], y, b5[u])) for u in range(NB)),
+    ]
     for c in range(2):
-        fin[c, :, 0:CA] = fin_a[c * 18 : c * 18 + 18]
-        fin[c, :, CA:] = fin_b[c * 18 : c * 18 + 18]
+        for (first, width), total in sums:
+            fin[c, :, first : first + width] = total[c * 18 : c * 18 + 18]
     sf = fresh()
 
     def hand_over(src, dst):
@@ -573,10 +594,10 @@
         ((2, 2, 32, D), BF16), ((2, 2, 32, D), BF16), ((2, 2, 64, D), BF16),
         ((64, D), BF16), ((64, D), F32), ((64, 1), F32), ((8, 8, D), BF16), ((8, 8, D), BF16),
         ((ROWS, D), BF16), ((3, ROWS, 256), BF16), ((3, 256, FQ), BF16),
-        ((4, 8, SLAB, CA), BF16), ((2, 4, SLAB, CA), BF16), ((2, 4, SLAB, CA), BF16), ((2, 8, SLAB, CA), BF16),
-        ((8, SLAB, CA), BF16), ((7, SLAB, CA), BF16),
-        ((8, 4, SLAB, CB), BF16), ((4, 2, SLAB, CB), BF16), ((3, 4, 2, SLAB, CB), BF16), ((3, 4, 2, SLAB, CB), BF16),
-        ((4, SLAB, CB), BF16), ((3, SLAB, CB), BF16),
+        ((2, 4, 8, SLAB, CA2), BF16), ((2, 2, 4, SLAB, CA2), BF16), ((2, 2, 4, SLAB, CA2), BF16), ((2, 2, 8, SLAB, CA2), BF16),
+        ((2, 8, SLAB, CA2), BF16), ((2, 7, SLAB, CA2), BF16),
+        ((NB, 8, 144, 128), BF16), ((NB, 2, 144, 128), BF16), ((3, NB, 2, 144, 128), BF16), ((3, NB, 2, 144, 128), BF16),
+        ((NB, 4, SLAB, 128), BF16), ((NB, 3, SLAB, 128), BF16),
         ((2, 18, FQ), F32),
     ]
     scratch = [pltpu.VMEM(shape, kind) for shape, kind in shapes]

time: 89.6 us -> 87.8 us (0.980); the launches traced: 88.2 us -> 87.6 us
  no operation moved by 1% of the time
where the time goes in v5:
time: 87.8 us; the launch traced here: 87.6 us
  Pallas kernels  86.8 us (99%)
    pallas_call x1, Pallas kernels, local(): pl.pallas_call(kernel, out_shape=results, in_specs=[anywhere, vmem, anywh...  84.6 us
    pallas_call x1, Pallas kernels, local(): pl.pallas_call(place, out_shape=results, in_specs=[anywhere] * 4, out_spe...  2.25 us

profile of v5, /device:TPU:1, one launch (start us, length us, event | category | flops | bytes accessed | tf_op | source)
XLA Modules:
  0.0 87.6 jit_solution(15429599848436789285)
XLA Ops:
  0.6 84.6 %shard_map.111 = (bf16[32,8,1152]{2,1,0:T(8,128)(2,1)}, bf16[32,8,1152]{2,1,0:T(8,128)(2,1)}, f32[18,1152]{1,0:T(8,128)}, f32[18,1152]{1,0:T(8,128)}) custom-call(bf16[32,8,1152]{2,1,0:T(8,128)(2,1)} %bitcast.8, f32[1152]{0:T(1024)} %gain1.1, bf16[864,1152]{1,0:T(8,128)(2,1)} %bitcast.7, bf16[288,1152]{1,0:T(8,128)(2,1)} %wo_h.1, f32[1152]{0:T(1024)} %gain2.1, ...), custom_call_target="tpu_custom_call" | custom-call | tf_op jit(solution)/shard_map/pallas_call | solution.py:615
  85.2 2.3 %shard_map.112 = (bf16[32,8,1152]{2,1,0:T(8,128)(2,1)}, bf16[32,8,1152]{2,1,0:T(8,128)(2,1)}, f32[18,1152]{1,0:T(8,128)}, f32[18,1152]{1,0:T(8,128)}) custom-call(bf16[32,8,1152]{2,1,0:T(8,128)(2,1)} %get-tuple-element.12.refs_0_, bf16[32,8,1152]{2,1,0:T(8,128)(2,1)} %get-tuple-element.13.refs_1_, f32[18,1152]{1,0:T(8,128)} %get-tuple-element.14.refs_2_, ...), custom_call_target="tpu_custom_call" | custom-call | tf_op jit(solution)/shard_map/pallas_call | solution.py:634

commit v6 on v5

--- a/solution.py
+++ b/solution.py
@@ -18,12 +18,12 @@
 QC = 288
 SLAB = 36
 ROWS = 32 * SLAB
-CA = 512
-CB = 640
-CA2 = CA // 2
+CA = 640
+CB = 512
+NA = CA // 128
 NB = CB // 128
 EPS = 1e-06
-N_SEM = 224
+N_SEM = 256
 
 
 def slab_sources(first, count):
@@ -55,7 +55,7 @@
     hl, gs, hres, wq, wo, w1, w2, na, qkv, qrec, att, arec, gflat, ga, nb,
     pf, pb, xr1, xs2, xq, mid, xhat, inv2, bo, go,
     perm, lbuf, rbuf,
-    wa, ya1, yas, yaq, ra, raq,
+    wa, ya1, yas, yaq, rp, zp1, zps, zpq, ra, raq,
     wb, zb1, zbs, zbq, rb, rbq, fin,
     ssem, rsem, lsem, gsem, osem, asem,
 ):
@@ -370,43 +370,59 @@
         rows = pl.ds(pl.multiple_of(i * 288, 32), 288)
         value = nn(lbuf[kept, rows, :], rbuf[kept, :, :CA]) + nn(lbuf[2, rows, :], rbuf[2, :, :CA])
         for m in range(8):
-            for u in range(2):
-                part = value[m * SLAB : (m + 1) * SLAB, u * CA2 : (u + 1) * CA2]
+            for u in range(NA):
+                part = value[m * SLAB : (m + 1) * SLAB, u * 128 : (u + 1) * 128]
                 wa[u, m % 4, i * 2 + m // 4] = part.astype(BF16)
         return carry
 
     def add(a, b):
         return (a.astype(F32) + b.astype(F32)).astype(BF16)
 
-    halves = (pl.ds(0, 80), pl.ds(80, 64))
-
-    def b_first(u):
-        far = wrap(zz + 4, 8)
-        return [
-            send(wb.at[u, far, halves[d]], zb1.at[u, d, halves[d]], z_dev(1 - 2 * d)) for d in range(2)
-        ]
-
-    def b_step(n, u, copies):
+    def ring_first(rows, halves, first):
+        far = rows(wrap(zz + 4, 8))
+        return [send(far.at[halves[d]], first.at[d, halves[d]], z_dev(1 - 2 * d)) for d in range(2)]
+
+    def ring_step(n, rows, halves, buffers, copies):
+        first, passed, got = buffers
         result = []
         for d in range(2):
             sign = 1 - 2 * d
-            chunk = wrap(zz + sign * (3 - n), 8)
+            chunk = rows(wrap(zz + sign * (3 - n), 8))
             copies[d].wait_recv()
             if n == 0:
-                taken, other = (slice(0, 80), slice(80, 144))[:: 1 - 2 * d]
-                zbs[n, u, d, taken, :] = add(wb[u, chunk, taken, :], zb1[u, d, taken, :])
-                zbs[n, u, d, other, :] = wb[u, chunk, other, :]
+                taken, other = halves[d], halves[1 - d]
+                passed[0, d, taken] = add(chunk[taken], first[d, taken])
+                passed[0, d, other] = chunk[other]
             else:
-                zbs[n, u, d] = add(wb[u, chunk], zbq[n - 1, u, d])
-            result.append(send(zbs.at[n, u, d], zbq.at[n, u, d], z_dev(sign)))
+                passed[n, d] = add(chunk[...], got[n - 1, d])
+            result.append(send(passed.at[n, d], got.at[n, d], z_dev(sign)))
         return result
 
-    def b_last(u, copies):
+    def ring_last(rows, buffers, copies):
         for copy in copies:
             copy.wait_recv()
-        total = wb[u, zz].astype(F32) + zbq[2, u, 0].astype(F32) + zbq[2, u, 1].astype(F32)
+        got = buffers[2]
+        return rows(zz)[...].astype(F32) + got[2, 0].astype(F32) + got[2, 1].astype(F32)
+
+    b_halves = (pl.ds(0, 80), pl.ds(80, 64))
+
+    def b_rows(u):
+        return lambda chunk: wb.at[u, chunk]
+
+    def b_buffers(u):
+        return zb1.at[u], zbs.at[u], zbq.at[u]
+
+    def b_steps(n, copies):
+        return [ring_step(n, b_rows(u), b_halves, b_buffers(u), copies[u]) for u in range(NB)]
+
+    def b_last(u, copies):
+        total = ring_last(b_rows(u), b_buffers(u), copies)
         for i in range(4):
             rb[u, i] = total[i * SLAB : (i + 1) * SLAB].astype(BF16)
+
+    p_halves = (pl.ds(0, 1), pl.ds(1, 1))
+    p_rows = lambda chunk: rp.at[chunk]
+    p_buffers = zp1, zps, zpq
 
     def a_first(u):
         far, up, down = wrap(y + 2, 4), wrap(y + 1, 4), wrap(y - 1, 4)
@@ -444,7 +460,10 @@
 
         def body(i, carry):
             total = wa[u, y, i].astype(F32) + yaq[u, 0, i].astype(F32) + yaq[u, 1, i].astype(F32)
-            ra[u, i] = total.astype(BF16)
+            if u < 2:
+                rp[i, u] = total.astype(BF16)
+            else:
+                ra[u - 2, i] = total.astype(BF16)
             return carry
 
         lax.fori_loop(0, 8, body, 0)
@@ -463,17 +482,21 @@
         return total
 
     lax.fori_loop(0, 4, grad_a, 0)
-    a1 = [a_first(u) for u in range(2)]
+    a1 = [a_first(u) for u in range(3)]
     lax.fori_loop(0, 4, grad_b, 0)
-    b1 = [b_first(u) for u in range(NB)]
+    b1 = [ring_first(b_rows(u), b_halves, zb1.at[u]) for u in range(NB)]
     partial_sums(1, lambda n: nt(rbuf[1], w1[n * 384 : n * 384 + 384, :]))
     e_first = reduce_first(1)
     d_second = reduce_second(0, d_first)
-    b2 = [b_step(0, u, b1[u]) for u in range(NB)]
     a2 = [a_second(0, a1[0])]
+    a1.append(a_first(3))
+    b2 = b_steps(0, b1)
+    a2.append(a_second(1, a1[1]))
+    a1.append(a_first(4))
     e_second = reduce_second(1, e_first)
-    a2.append(a_second(1, a1[1]))
-    b3 = [b_step(1, u, b2[u]) for u in range(NB)]
+    b3 = b_steps(1, b2)
+    a2.append(a_second(2, a1[2]))
+    a_last(0, a2[0])
 
     def out_view(ref):
         return lambda plane, a: ref.at[pl.ds(peer_seq(plane, a, 0), 2)]
@@ -489,7 +512,10 @@
     down_rows = reduce_third(0, d_second)
     bo[...] = (mid[...].astype(F32) + down_rows).reshape(8, 8, D).astype(BF16)
     o_first = give(bo, out_b, 0)
-    b4 = [b_step(2, u, b3[u]) for u in range(NB)]
+    b4 = b_steps(2, b3)
+    a2.append(a_second(3, a1[3]))
+    a_last(1, a2[1])
+    p1 = ring_first(p_rows, p_halves, zp1)
 
     scaled = reduce_third(1, e_second) * g2
     x_hat2 = xhat[...]
@@ -499,23 +525,32 @@
     go[...] = (upstream + inv2[...] * (scaled - plain - x_hat2 * cross)).reshape(8, 8, D).astype(BF16)
     m_first = give(go, out_g, 4)
 
-    a3 = []
-    for u in range(2):
+    a2.append(a_second(4, a1[4]))
+    p2 = ring_step(0, p_rows, p_halves, p_buffers, p1)
+    a3 = {}
+
+    def a_finish(u):
         a_last(u, a2[u])
-        a3.append(straight(ra.at[u], raq.at[u], z_dev, zz, 8))
+        a3[u] = straight(ra.at[u - 2], raq.at[u - 2], z_dev, zz, 8)
+
+    a_finish(2)
     o_further = gather_second(out_view(out_b), o_first)
+    a_finish(3)
+    p3 = ring_step(1, p_rows, p_halves, p_buffers, p2)
+    a_finish(4)
     b5 = []
     for u in range(NB):
         b_last(u, b4[u])
         b5.append(straight(rb.at[u], rbq.at[u], y_dev, y, 4))
+    p4 = ring_step(2, p_rows, p_halves, p_buffers, p3)
     m_further = gather_second(out_view(out_g), m_first)
-    sums = [
-        *(((u * CA2, CA2), straight_sum(ra.at[u], raq.at[u], zz, a3[u])) for u in range(2)),
-        *(((CA + u * 128, 128), straight_sum(rb.at[u], rbq.at[u], y, b5[u])) for u in range(NB)),
-    ]
+    sums = [(CA + u * 128, straight_sum(rb.at[u], rbq.at[u], y, b5[u])) for u in range(NB)]
+    sums += [(u * 128, straight_sum(ra.at[u - 2], raq.at[u - 2], zz, a3[u])) for u in range(2, NA)]
+    pair = ring_last(p_rows, p_buffers, p4)
+    sums += [(u * 128, pair[u]) for u in range(2)]
     for c in range(2):
-        for (first, width), total in sums:
-            fin[c, :, first : first + width] = total[c * 18 : c * 18 + 18]
+        for first, total in sums:
+            fin[c, :, first : first + 128] = total[c * 18 : c * 18 + 18]
     sf = fresh()
 
     def hand_over(src, dst):
@@ -594,9 +629,13 @@
         ((2, 2, 32, D), BF16), ((2, 2, 32, D), BF16), ((2, 2, 64, D), BF16),
         ((64, D), BF16), ((64, D), F32), ((64, 1), F32), ((8, 8, D), BF16), ((8, 8, D), BF16),
         ((ROWS, D), BF16), ((3, ROWS, 256), BF16), ((3, 256, FQ), BF16),
-        ((2, 4, 8, SLAB, CA2), BF16), ((2, 2, 4, SLAB, CA2), BF16), ((2, 2, 4, SLAB, CA2), BF16), ((2, 2, 8, SLAB, CA2), BF16),
-        ((2, 8, SLAB, CA2), BF16), ((2, 7, SLAB, CA2), BF16),
-        ((NB, 8, 144, 128), BF16), ((NB, 2, 144, 128), BF16), ((3, NB, 2, 144, 128), BF16), ((3, NB, 2, 144, 128), BF16),
+        ((NA, 4, 8, SLAB, 128), BF16), ((NA, 2, 4, SLAB, 128), BF16),
+        ((NA, 2, 4, SLAB, 128), BF16), ((NA, 2, 8, SLAB, 128), BF16),
+        ((8, 2, SLAB, 128), BF16), ((2, 2, SLAB, 128), BF16),
+        ((3, 2, 2, SLAB, 128), BF16), ((3, 2, 2, SLAB, 128), BF16),
+        ((NA - 2, 8, SLAB, 128), BF16), ((NA - 2, 7, SLAB, 128), BF16),
+        ((NB, 8, 144, 128), BF16), ((NB, 2, 144, 128), BF16),
+        ((NB, 3, 2, 144, 128), BF16), ((NB, 3, 2, 144, 128), BF16),
         ((NB, 4, SLAB, 128), BF16), ((NB, 3, SLAB, 128), BF16),
         ((2, 18, FQ), F32),
     ]

time: 87.8 us -> 90.6 us (1.032)
  Pallas kernels: 86.8 us -> 89.5 us
    pallas_call x1, Pallas kernels: 84.6 us -> 87.2 us  [local(): pl.pallas_call(kernel, out_shape=results, in_specs=[anywhere, vmem, anywh...]
where the time goes in v6:
time: 90.6 us; the launch traced here: 90.3 us
  Pallas kernels  89.5 us (99%)
    pallas_call x1, Pallas kernels, local(): pl.pallas_call(kernel, out_shape=results, in_specs=[anywhere, vmem, anywh...  87.2 us
    pallas_call x1, Pallas kernels, local(): pl.pallas_call(place, out_shape=results, in_specs=[anywhere] * 4, out_spe...  2.25 us

profile of v6, /device:TPU:1, one launch (start us, length us, event | category | flops | bytes accessed | tf_op | source)
XLA Modules:
  0.0 90.3 jit_solution(17046156425210465205)
XLA Ops:
  0.6 87.2 %shard_map.111 = (bf16[32,8,1152]{2,1,0:T(8,128)(2,1)}, bf16[32,8,1152]{2,1,0:T(8,128)(2,1)}, f32[18,1152]{1,0:T(8,128)}, f32[18,1152]{1,0:T(8,128)}) custom-call(bf16[32,8,1152]{2,1,0:T(8,128)(2,1)} %bitcast.8, f32[1152]{0:T(1024)} %gain1.1, bf16[864,1152]{1,0:T(8,128)(2,1)} %bitcast.7, bf16[288,1152]{1,0:T(8,128)(2,1)} %wo_h.1, f32[1152]{0:T(1024)} %gain2.1, ...), custom_call_target="tpu_custom_call" | custom-call | tf_op jit(solution)/shard_map/pallas_call | solution.py:654
  87.9 2.3 %shard_map.112 = (bf16[32,8,1152]{2,1,0:T(8,128)(2,1)}, bf16[32,8,1152]{2,1,0:T(8,128)(2,1)}, f32[18,1152]{1,0:T(8,128)}, f32[18,1152]{1,0:T(8,128)}) custom-call(bf16[32,8,1152]{2,1,0:T(8,128)(2,1)} %get-tuple-element.12.refs_0_, bf16[32,8,1152]{2,1,0:T(8,128)(2,1)} %get-tuple-element.13.refs_1_, f32[18,1152]{1,0:T(8,128)} %get-tuple-element.14.refs_2_, ...), custom_call_target="tpu_custom_call" | custom-call | tf_op jit(solution)/shard_map/pallas_call | solution.py:673

commit v7 on v5

--- a/solution.py
+++ b/solution.py
@@ -134,6 +134,11 @@
         copy.start()
         started.append(copy)
         return copy
+
+    def sent():
+        for copy in started:
+            copy.wait_send()
+        started.clear()
 
     base_h, base_m = fresh(32), fresh(32)
 
@@ -325,12 +330,25 @@
     def quarter(ref):
         return lambda plane, a: ref.at[plane, pl.ds(a * 16, 16)]
 
+    early = list(started)
+    started.clear()
     n_first = gather_first(quarter(nb), lambda a: quarter(nb)(t, a))
 
     for n in range(3):
         c = slice(n * 384, n * 384 + 384)
         lbuf[0, c, :] = nt(perm[c, :], g_all).astype(BF16)
+    for other in range(32):
+
+        @pl.when(s != other)
+        def _():
+            to_patches(other).wait_send()
+
+        @pl.when(jnp.logical_not(jnp.logical_and(s == other, plane_of(other) == t)))
+        def _():
+            to_frame(other).wait_send()
     n_further = gather_second(quarter(nb), n_first)
+    for copy in early:
+        copy.wait_send()
     gather_third(n_further)
     nb_all = nb[...].reshape(256, D)
     for n in range(3):
@@ -489,6 +507,9 @@
     down_rows = reduce_third(0, d_second)
     bo[...] = (mid[...].astype(F32) + down_rows).reshape(8, 8, D).astype(BF16)
     o_first = give(bo, out_b, 0)
+    a3 = []
+    a_last(0, a2[0])
+    a3.append(straight(ra.at[0], raq.at[0], z_dev, zz, 8))
     b4 = [b_step(2, u, b3[u]) for u in range(NB)]
 
     scaled = reduce_third(1, e_second) * g2
@@ -499,16 +520,15 @@
     go[...] = (upstream + inv2[...] * (scaled - plain - x_hat2 * cross)).reshape(8, 8, D).astype(BF16)
     m_first = give(go, out_g, 4)
 
-    a3 = []
-    for u in range(2):
-        a_last(u, a2[u])
-        a3.append(straight(ra.at[u], raq.at[u], z_dev, zz, 8))
+    a_last(1, a2[1])
+    a3.append(straight(ra.at[1], raq.at[1], z_dev, zz, 8))
     o_further = gather_second(out_view(out_b), o_first)
     b5 = []
     for u in range(NB):
         b_last(u, b4[u])
         b5.append(straight(rb.at[u], rbq.at[u], y_dev, y, 4))
     m_further = gather_second(out_view(out_g), m_first)
+    sent()
     sums = [
         *(((u * CA2, CA2), straight_sum(ra.at[u], raq.at[u], zz, a3[u])) for u in range(2)),
         *(((CA + u * 128, 128), straight_sum(rb.at[u], rbq.at[u], y, b5[u])) for u in range(NB)),
@@ -544,18 +564,7 @@
     for copy in placed:
         copy.wait()
 
-    for other in range(32):
-
-        @pl.when(s != other)
-        def _():
-            to_patches(other).wait_send()
-
-        @pl.when(jnp.logical_not(jnp.logical_and(s == other, plane_of(other) == t)))
-        def _():
-            to_frame(other).wait_send()
-
-    for copy in started:
-        copy.wait_send()
+    sent()
 
 
 def place(*refs):

time: 87.8 us -> 88.5 us (level)
  no operation moved by 1% of the time
where the time goes in v7:
time: 88.5 us; the launch traced here: 88.3 us
  Pallas kernels  87.5 us (99%)
    pallas_call x1, Pallas kernels, local(): pl.pallas_call(kernel, out_shape=results, in_specs=[anywhere, vmem, anywh...  85.2 us
    pallas_call x1, Pallas kernels, local(): pl.pallas_call(place, out_shape=results, in_specs=[anywhere] * 4, out_spe...  2.25 us

profile of v7, /device:TPU:1, one launch (start us, length us, event | category | flops | bytes accessed | tf_op | source)
XLA Modules:
  0.0 88.3 jit_solution(10744160787716430126)
XLA Ops:
  0.6 85.2 %shard_map.111 = (bf16[32,8,1152]{2,1,0:T(8,128)(2,1)}, bf16[32,8,1152]{2,1,0:T(8,128)(2,1)}, f32[18,1152]{1,0:T(8,128)}, f32[18,1152]{1,0:T(8,128)}) custom-call(bf16[32,8,1152]{2,1,0:T(8,128)(2,1)} %bitcast.8, f32[1152]{0:T(1024)} %gain1.1, bf16[864,1152]{1,0:T(8,128)(2,1)} %bitcast.7, bf16[288,1152]{1,0:T(8,128)(2,1)} %wo_h.1, f32[1152]{0:T(1024)} %gain2.1, ...), custom_call_target="tpu_custom_call" | custom-call | tf_op jit(solution)/shard_map/pallas_call | solution.py:624
  85.9 2.3 %shard_map.112 = (bf16[32,8,1152]{2,1,0:T(8,128)(2,1)}, bf16[32,8,1152]{2,1,0:T(8,128)(2,1)}, f32[18,1152]{1,0:T(8,128)}, f32[18,1152]{1,0:T(8,128)}) custom-call(bf16[32,8,1152]{2,1,0:T(8,128)(2,1)} %get-tuple-element.12.refs_0_, bf16[32,8,1152]{2,1,0:T(8,128)(2,1)} %get-tuple-element.13.refs_1_, f32[18,1152]{1,0:T(8,128)} %get-tuple-element.14.refs_2_, ...), custom_call_target="tpu_custom_call" | custom-call | tf_op jit(solution)/shard_map/pallas_call | solution.py:643

commit v8 on v5

--- a/solution.py
+++ b/solution.py
@@ -331,27 +331,32 @@
         c = slice(n * 384, n * 384 + 384)
         lbuf[0, c, :] = nt(perm[c, :], g_all).astype(BF16)
     n_further = gather_second(quarter(nb), n_first)
-    gather_third(n_further)
-    nb_all = nb[...].reshape(256, D)
-    for n in range(3):
-        c = slice(n * 384, n * 384 + 384)
-        lbuf[1, c, :] = nt(perm[c, :], nb_all).astype(BF16)
-
-    swapped = [send(lbuf.at[core], lbuf.at[2], core_dev)]
+
+    swapped = []
     kept = 1 - core
-
     root = (2.0 / np.pi) ** 0.5
-    for n in range(3):
-        c = slice(n * 384, n * 384 + 384)
-        pre = nn(nb_all, w1[:, c])
-        square = pre * pre
-        th = jnp.tanh(root * (pre + 0.044715 * (square * pre)))
-        half = 0.5 * (1.0 + th)
-        rbuf[0, :, c] = (pre * half).astype(BF16)
-        slope = half + 0.5 * pre * (1.0 - th * th) * (root * (1.0 + 3 * 0.044715 * square))
-        rbuf[1, :, c] = (ga[:, c] * slope).astype(BF16)
-        part = pl.ds(n * 384, 384)
-        swapped.append(send(rbuf.at[core, :, part], rbuf.at[2, :, part], core_dev))
+    for part in range(2):
+        if part:
+            gather_third(n_further)
+        pair = lax.rem(t // 2 + part, 2)
+        rows = pl.ds(pl.multiple_of(pair * 128, 128), 128)
+        nb_pair = nb[pl.ds(pair * 2, 2)].reshape(128, D)
+        for n in range(3):
+            c = slice(n * 384, n * 384 + 384)
+            lbuf[1, c, rows] = nt(perm[c, :], nb_pair).astype(BF16)
+        if part:
+            swapped.append(send(lbuf.at[core], lbuf.at[2], core_dev))
+        for n in range(3):
+            c = slice(n * 384, n * 384 + 384)
+            pre = nn(nb_pair, w1[:, c])
+            square = pre * pre
+            th = jnp.tanh(root * (pre + 0.044715 * (square * pre)))
+            half = 0.5 * (1.0 + th)
+            rbuf[0, rows, c] = (pre * half).astype(BF16)
+            slope = half + 0.5 * pre * (1.0 - th * th) * (root * (1.0 + 3 * 0.044715 * square))
+            rbuf[1, rows, c] = (ga[rows, c] * slope).astype(BF16)
+            lanes = pl.ds(n * 384, 384)
+            swapped.append(send(rbuf.at[core, rows, lanes], rbuf.at[2, rows, lanes], core_dev))
 
     partial_sums(0, lambda n: nt(rbuf[0], w2[n * 384 : n * 384 + 384, :]))
     d_first = reduce_first(0)

time: 87.8 us -> 87.9 us (level)
  no operation moved by 1% of the time
where the time goes in v8:
time: 87.9 us; the launch traced here: 87.7 us
  Pallas kernels  86.9 us (99%)
    pallas_call x1, Pallas kernels, local(): pl.pallas_call(kernel, out_shape=results, in_specs=[anywhere, vmem, anywh...  84.7 us
    pallas_call x1, Pallas kernels, local(): pl.pallas_call(place, out_shape=results, in_specs=[anywhere] * 4, out_spe...  2.25 us

profile of v8, /device:TPU:1, one launch (start us, length us, event | category | flops | bytes accessed | tf_op | source)
XLA Modules:
  0.0 87.7 jit_solution(3878392338007597173)
XLA Ops:
  0.6 84.7 %shard_map.111 = (bf16[32,8,1152]{2,1,0:T(8,128)(2,1)}, bf16[32,8,1152]{2,1,0:T(8,128)(2,1)}, f32[18,1152]{1,0:T(8,128)}, f32[18,1152]{1,0:T(8,128)}) custom-call(bf16[32,8,1152]{2,1,0:T(8,128)(2,1)} %bitcast.8, f32[1152]{0:T(1024)} %gain1.1, bf16[864,1152]{1,0:T(8,128)(2,1)} %bitcast.7, bf16[288,1152]{1,0:T(8,128)(2,1)} %wo_h.1, f32[1152]{0:T(1024)} %gain2.1, ...), custom_call_target="tpu_custom_call" | custom-call | tf_op jit(solution)/shard_map/pallas_call | solution.py:620
  85.3 2.3 %shard_map.112 = (bf16[32,8,1152]{2,1,0:T(8,128)(2,1)}, bf16[32,8,1152]{2,1,0:T(8,128)(2,1)}, f32[18,1152]{1,0:T(8,128)}, f32[18,1152]{1,0:T(8,128)}) custom-call(bf16[32,8,1152]{2,1,0:T(8,128)(2,1)} %get-tuple-element.12.refs_0_, bf16[32,8,1152]{2,1,0:T(8,128)(2,1)} %get-tuple-element.13.refs_1_, f32[18,1152]{1,0:T(8,128)} %get-tuple-element.14.refs_2_, ...), custom_call_target="tpu_custom_call" | custom-call | tf_op jit(solution)/shard_map/pallas_call | solution.py:639

commit v9 on v8

--- a/solution.py
+++ b/solution.py
@@ -137,21 +137,18 @@
 
     base_h, base_m = fresh(32), fresh(32)
 
-    def to_patches(other):
+    turns = (*range(16, 24), *range(8, 16), *range(24, 32), *range(1, 8))
+
+    def to_patches(turn):
+        other = lax.rem(s + turn, 32)
         return pltpu.make_async_remote_copy(
-            src_ref=qkv.at[other], dst_ref=qrec.at[s], send_sem=ssem.at[base_h + other], recv_sem=rsem.at[base_h + s],
+            src_ref=qkv.at[other], dst_ref=qrec.at[s], send_sem=ssem.at[base_h + turn], recv_sem=rsem.at[base_h + s],
             device_id={"seq": other}, device_id_type=MESH,
         )
 
-    for other in range(32):
-
-        @pl.when(s != other)
-        def _():
-            to_patches(other).start()
-
-        @pl.when(s == other)
-        def _():
-            pltpu.make_async_copy(qkv.at[other], qrec.at[other], rsem.at[base_h + other]).start()
+    for turn in turns:
+        to_patches(turn).start()
+    pltpu.make_async_copy(qkv.at[s], qrec.at[s], rsem.at[base_h + s]).start()
 
     turned = [
         pltpu.make_async_copy(
@@ -241,24 +238,26 @@
     def plane_of(frame):
         return lax.rem(frame // 8 + frame // 2 % 4 + zh + y, 4)
 
-    def to_frame(frame):
+    def to_frame(turn):
+        frame = lax.rem(s + turn, 32)
         return pltpu.make_async_remote_copy(
             src_ref=att.at[frame], dst_ref=arec.at[t, zh * 2 + core],
-            send_sem=ssem.at[base_m + frame], recv_sem=rsem.at[base_m + t * 8 + zh * 2 + core],
+            send_sem=ssem.at[base_m + turn], recv_sem=rsem.at[base_m + t * 8 + zh * 2 + core],
             device_id={"seq": frame, "tensor": plane_of(frame)}, device_id_type=MESH,
         )
 
-    for frame in range(32):
-        stays = jnp.logical_and(s == frame, plane_of(frame) == t)
-
-        @pl.when(jnp.logical_not(stays))
-        def _():
-            to_frame(frame).start()
-
-        @pl.when(stays)
-        def _():
-            here = arec.at[t, zh * 2 + core]
-            pltpu.make_async_copy(att.at[frame], here, rsem.at[base_m + t * 8 + zh * 2 + core]).start()
+    for turn in turns:
+        to_frame(turn).start()
+    stays = plane_of(s) == t
+
+    @pl.when(jnp.logical_not(stays))
+    def _():
+        to_frame(0).start()
+
+    @pl.when(stays)
+    def _():
+        here = arec.at[t, zh * 2 + core]
+        pltpu.make_async_copy(att.at[s], here, rsem.at[base_m + t * 8 + zh * 2 + core]).start()
 
     for copy in wo_further:
         copy.wait_recv()
@@ -549,15 +548,13 @@
     for copy in placed:
         copy.wait()
 
-    for other in range(32):
-
-        @pl.when(s != other)
-        def _():
-            to_patches(other).wait_send()
-
-        @pl.when(jnp.logical_not(jnp.logical_and(s == other, plane_of(other) == t)))
-        def _():
-            to_frame(other).wait_send()
+    for turn in turns:
+        to_patches(turn).wait_send()
+        to_frame(turn).wait_send()
+
+    @pl.when(jnp.logical_not(stays))
+    def _():
+        to_frame(0).wait_send()
 
     for copy in started:
         copy.wait_send()

time: 87.9 us -> 87.9 us (level)
  no operation moved by 1% of the time
where the time goes in v9:
time: 87.9 us; the launch traced here: 87.7 us
  Pallas kernels  86.9 us (99%)
    pallas_call x1, Pallas kernels, local(): pl.pallas_call(kernel, out_shape=results, in_specs=[anywhere, vmem, anywh...  84.7 us
    pallas_call x1, Pallas kernels, local(): pl.pallas_call(place, out_shape=results, in_specs=[anywhere] * 4, out_spe...  2.25 us

profile of v9, /device:TPU:1, one launch (start us, length us, event | category | flops | bytes accessed | tf_op | source)
XLA Modules:
  0.0 87.7 jit_solution(9864013936543688045)
XLA Ops:
  0.6 84.7 %shard_map.111 = (bf16[32,8,1152]{2,1,0:T(8,128)(2,1)}, bf16[32,8,1152]{2,1,0:T(8,128)(2,1)}, f32[18,1152]{1,0:T(8,128)}, f32[18,1152]{1,0:T(8,128)}) custom-call(bf16[32,8,1152]{2,1,0:T(8,128)(2,1)} %bitcast.8, f32[1152]{0:T(1024)} %gain1.1, bf16[864,1152]{1,0:T(8,128)(2,1)} %bitcast.7, bf16[288,1152]{1,0:T(8,128)(2,1)} %wo_h.1, f32[1152]{0:T(1024)} %gain2.1, ...), custom_call_target="tpu_custom_call" | custom-call | tf_op jit(solution)/shard_map/pallas_call | solution.py:617
  85.3 2.3 %shard_map.112 = (bf16[32,8,1152]{2,1,0:T(8,128)(2,1)}, bf16[32,8,1152]{2,1,0:T(8,128)(2,1)}, f32[18,1152]{1,0:T(8,128)}, f32[18,1152]{1,0:T(8,128)}) custom-call(bf16[32,8,1152]{2,1,0:T(8,128)(2,1)} %get-tuple-element.12.refs_0_, bf16[32,8,1152]{2,1,0:T(8,128)(2,1)} %get-tuple-element.13.refs_1_, f32[18,1152]{1,0:T(8,128)} %get-tuple-element.14.refs_2_, ...), custom_call_target="tpu_custom_call" | custom-call | tf_op jit(solution)/shard_map/pallas_call | solution.py:636

commit v10 on v9

--- a/solution.py
+++ b/solution.py
@@ -466,10 +466,10 @@
             total = total + received[i].astype(F32)
         return total
 
+    lax.fori_loop(0, 4, grad_b, 0)
+    b1 = [b_first(u) for u in range(NB)]
     lax.fori_loop(0, 4, grad_a, 0)
     a1 = [a_first(u) for u in range(2)]
-    lax.fori_loop(0, 4, grad_b, 0)
-    b1 = [b_first(u) for u in range(NB)]
     partial_sums(1, lambda n: nt(rbuf[1], w1[n * 384 : n * 384 + 384, :]))
     e_first = reduce_first(1)
     d_second = reduce_second(0, d_first)

time: 87.9 us -> 88.9 us (1.011)
  Pallas kernels: 86.9 us -> 88 us
    pallas_call x1, Pallas kernels: 84.7 us -> 85.7 us  [local(): pl.pallas_call(kernel, out_shape=results, in_specs=[anywhere, vmem, anywh...]
where the time goes in v10:
time: 88.9 us; the launch traced here: 88.8 us
  Pallas kernels  88 us (99%)
    pallas_call x1, Pallas kernels, local(): pl.pallas_call(kernel, out_shape=results, in_specs=[anywhere, vmem, anywh...  85.7 us
    pallas_call x1, Pallas kernels, local(): pl.pallas_call(place, out_shape=results, in_specs=[anywhere] * 4, out_spe...  2.25 us

profile of v10, /device:TPU:1, one launch (start us, length us, event | category | flops | bytes accessed | tf_op | source)
XLA Modules:
  0.0 88.8 jit_solution(320719089377553122)
XLA Ops:
  0.6 85.7 %shard_map.111 = (bf16[32,8,1152]{2,1,0:T(8,128)(2,1)}, bf16[32,8,1152]{2,1,0:T(8,128)(2,1)}, f32[18,1152]{1,0:T(8,128)}, f32[18,1152]{1,0:T(8,128)}) custom-call(bf16[32,8,1152]{2,1,0:T(8,128)(2,1)} %bitcast.8, f32[1152]{0:T(1024)} %gain1.1, bf16[864,1152]{1,0:T(8,128)(2,1)} %bitcast.7, bf16[288,1152]{1,0:T(8,128)(2,1)} %wo_h.1, f32[1152]{0:T(1024)} %gain2.1, ...), custom_call_target="tpu_custom_call" | custom-call | tf_op jit(solution)/shard_map/pallas_call | solution.py:617
  86.3 2.3 %shard_map.112 = (bf16[32,8,1152]{2,1,0:T(8,128)(2,1)}, bf16[32,8,1152]{2,1,0:T(8,128)(2,1)}, f32[18,1152]{1,0:T(8,128)}, f32[18,1152]{1,0:T(8,128)}) custom-call(bf16[32,8,1152]{2,1,0:T(8,128)(2,1)} %get-tuple-element.12.refs_0_, bf16[32,8,1152]{2,1,0:T(8,128)(2,1)} %get-tuple-element.13.refs_1_, f32[18,1152]{1,0:T(8,128)} %get-tuple-element.14.refs_2_, ...), custom_call_target="tpu_custom_call" | custom-call | tf_op jit(solution)/shard_map/pallas_call | solution.py:636

commit v11 on v9

--- a/solution.py
+++ b/solution.py
@@ -473,8 +473,8 @@
     partial_sums(1, lambda n: nt(rbuf[1], w1[n * 384 : n * 384 + 384, :]))
     e_first = reduce_first(1)
     d_second = reduce_second(0, d_first)
+    a2 = [a_second(0, a1[0])]
     b2 = [b_step(0, u, b1[u]) for u in range(NB)]
-    a2 = [a_second(0, a1[0])]
     e_second = reduce_second(1, e_first)
     a2.append(a_second(1, a1[1]))
     b3 = [b_step(1, u, b2[u]) for u in range(NB)]
@@ -493,6 +493,8 @@
     down_rows = reduce_third(0, d_second)
     bo[...] = (mid[...].astype(F32) + down_rows).reshape(8, 8, D).astype(BF16)
     o_first = give(bo, out_b, 0)
+    a_last(0, a2[0])
+    a3 = [straight(ra.at[0], raq.at[0], z_dev, zz, 8)]
     b4 = [b_step(2, u, b3[u]) for u in range(NB)]
 
     scaled = reduce_third(1, e_second) * g2
@@ -503,10 +505,8 @@
     go[...] = (upstream + inv2[...] * (scaled - plain - x_hat2 * cross)).reshape(8, 8, D).astype(BF16)
     m_first = give(go, out_g, 4)
 
-    a3 = []
-    for u in range(2):
-        a_last(u, a2[u])
-        a3.append(straight(ra.at[u], raq.at[u], z_dev, zz, 8))
+    a_last(1, a2[1])
+    a3.append(straight(ra.at[1], raq.at[1], z_dev, zz, 8))
     o_further = gather_second(out_view(out_b), o_first)
     b5 = []
     for u in range(NB):

time: 87.9 us -> 89.4 us (1.017)
  Pallas kernels: 86.9 us -> 88.4 us
    pallas_call x1, Pallas kernels: 84.7 us -> 86.1 us  [local(): pl.pallas_call(kernel, out_shape=results, in_specs=[anywhere, vmem, anywh...]
where the time goes in v11:
time: 89.4 us; the launch traced here: 89.2 us
  Pallas kernels  88.4 us (99%)
    pallas_call x1, Pallas kernels, local(): pl.pallas_call(kernel, out_shape=results, in_specs=[anywhere, vmem, anywh...  86.1 us
    pallas_call x1, Pallas kernels, local(): pl.pallas_call(place, out_shape=results, in_specs=[anywhere] * 4, out_spe...  2.25 us

profile of v11, /device:TPU:1, one launch (start us, length us, event | category | flops | bytes accessed | tf_op | source)
XLA Modules:
  0.0 89.2 jit_solution(18345946911964760878)
XLA Ops:
  0.6 86.1 %shard_map.111 = (bf16[32,8,1152]{2,1,0:T(8,128)(2,1)}, bf16[32,8,1152]{2,1,0:T(8,128)(2,1)}, f32[18,1152]{1,0:T(8,128)}, f32[18,1152]{1,0:T(8,128)}) custom-call(bf16[32,8,1152]{2,1,0:T(8,128)(2,1)} %bitcast.8, f32[1152]{0:T(1024)} %gain1.1, bf16[864,1152]{1,0:T(8,128)(2,1)} %bitcast.7, bf16[288,1152]{1,0:T(8,128)(2,1)} %wo_h.1, f32[1152]{0:T(1024)} %gain2.1, ...), custom_call_target="tpu_custom_call" | custom-call | tf_op jit(solution)/shard_map/pallas_call | solution.py:617
  86.8 2.3 %shard_map.112 = (bf16[32,8,1152]{2,1,0:T(8,128)(2,1)}, bf16[32,8,1152]{2,1,0:T(8,128)(2,1)}, f32[18,1152]{1,0:T(8,128)}, f32[18,1152]{1,0:T(8,128)}) custom-call(bf16[32,8,1152]{2,1,0:T(8,128)(2,1)} %get-tuple-element.12.refs_0_, bf16[32,8,1152]{2,1,0:T(8,128)(2,1)} %get-tuple-element.13.refs_1_, f32[18,1152]{1,0:T(8,128)} %get-tuple-element.14.refs_2_, ...), custom_call_target="tpu_custom_call" | custom-call | tf_op jit(solution)/shard_map/pallas_call | solution.py:636
